TPU v7x, 512 devices: a whole 4x4x16 slice. The times are simulated.
512 devices in a mesh: section: 8 (over x, core), seq: 16 (over z_hi, y), dp: 4 (over z_lo).
Axes of the slice: x: 4, y: 4, z: 16 (z_hi: 4, z_lo: 4; z = z_hi * 4 + z_lo), core: 2. Of those that a mesh axis runs over, the one named last changes fastest.
Arguments:
- frozen_queries: bfloat16 [8, 4, 2048, 4096], P('section', 'dp', 'seq'), may hold values from -128 to 128
- key_value_pairs: bfloat16 [8, 4, 2048, 1024], P('section', 'dp', 'seq'), may hold values from -8 to 8
- adapter_input: bfloat16 [8, 4, 2048, 64], P('section', 'dp', 'seq'), may hold values from -6 to 6
- adapter_up_matrix: bfloat16 [8, 64, 4096], P('section', None, 'seq'), may hold values from -0.75 to 0.75
- upstream: bfloat16 [8, 4, 2048, 4096], P('section', 'dp', 'seq'), may hold values from -6 to 6
- document_index: int32 [8, 4, 2048], P('section', 'dp'), may hold values from 0 to 15, as said below
Outputs:
- query_gradient: bfloat16 [8, 4, 2048, 4096], P('section', 'dp', 'seq')
- key_value_gradient: bfloat16 [8, 4, 2048, 1024], P('section', 'dp', 'seq')
- adapter_input_gradient: bfloat16 [8, 4, 2048, 64], P('section', 'dp', 'seq')
- adapter_up_gradient: float32 [8, 64, 4096], P('section', 'dp', 'seq')
Inputs may be any that keep to these rules, and one draw needn't show every extreme that they name: `document_index`: along each pack the numbers never fall; every number appears; every document spans at most 256 positions, and one document of each pack spans exactly that many.
All inputs are finite; a program needn't handle non-finite values.
Results may differ from a plain program's by a relative error of at most 0.014.
Values may be sent and summed in bfloat16 or wider, within the bound.
A program may use at most 64 MiB of HBM per device.

v0:
```python
import math

import jax
import jax.numpy as jnp
from jax import lax
from jax.sharding import PartitionSpec as P

QUERY_HEADS = 32
HK = 4
HEAD_SIZE = 128


def passed_along(value, axis, steps):
    count = lax.axis_size(axis)
    pairs = [(source, (source + steps) % count) for source in range(count)]
    return lax.ppermute(value, axis, pairs)


def contract_last(left, right):
    return lax.dot_general(
        left, right, (((1,), (1,)), ((), ())), preferred_element_type=jnp.float32
    )


def contract_first(left, right):
    return lax.dot_general(
        left, right, (((0,), (0,)), ((), ())), preferred_element_type=jnp.float32
    )


def per_device(
    frozen_queries, key_value_pairs, adapter_input, adapter_up_matrix, upstream, document_index
):
    groups = lax.axis_size("seq")
    local_heads = QUERY_HEADS // groups
    sharing = QUERY_HEADS // HK
    scale_factor = 1.0 / math.sqrt(HEAD_SIZE)
    cot_tokens = passed_along(upstream, "section", -1)
    query_split = lax.all_to_all(frozen_queries, "seq", split_axis=3, concat_axis=2, tiled=True)
    cot_split = lax.all_to_all(cot_tokens, "seq", split_axis=3, concat_axis=2, tiled=True)
    adapter_row_list = lax.all_gather(adapter_input, "seq", axis=2, tiled=True)[0, 0]
    pair_all = lax.all_gather(key_value_pairs, "seq", axis=2, tiled=True)
    pair_index = lax.axis_index("seq") * local_heads // sharing
    pair_local = lax.dynamic_slice_in_dim(pair_all, pair_index * 2 * HEAD_SIZE, 2 * HEAD_SIZE, 3)[
        0, 0
    ]
    local_adapter_part = adapter_up_matrix[0]
    query_values = (
        query_split[0, 0].astype(jnp.float32)
        + jnp.dot(adapter_row_list, local_adapter_part, preferred_element_type=jnp.float32)
    ).astype(jnp.bfloat16)
    cotangent_rows = cot_split[0, 0]
    document_numbers = document_index[0, 0]
    key_rows = pair_local[:, :HEAD_SIZE]
    value_rows = pair_local[:, HEAD_SIZE:]
    length = query_values.shape[0]
    block = length // 8
    positions = jnp.arange(length, dtype=jnp.int32)
    key_total = jnp.zeros((length, HEAD_SIZE), jnp.float32)
    value_total = jnp.zeros((length, HEAD_SIZE), jnp.float32)
    query_blocks = []
    for start_row in range(0, length, block):
        stop_row = start_row + block
        low_row = max(0, start_row - block)
        visible = (
            document_numbers[start_row:stop_row, None] == document_numbers[None, low_row:stop_row]
        ) & (positions[start_row:stop_row, None] >= positions[None, low_row:stop_row])
        seen_keys = key_rows[low_row:stop_row]
        seen_values = value_rows[low_row:stop_row]
        query_block = query_values[start_row:stop_row].reshape(block, local_heads, HEAD_SIZE)
        cot_block = cotangent_rows[start_row:stop_row].reshape(block, local_heads, HEAD_SIZE)
        scores = (
            jnp.einsum("qhd,kd->hqk", query_block, seen_keys, preferred_element_type=jnp.float32)
            * scale_factor
        )
        scores = jnp.where(visible[None], scores, -jnp.inf)
        shifted = jnp.exp(scores - jnp.max(scores, axis=2, keepdims=True))
        probs = shifted / jnp.sum(shifted, axis=2, keepdims=True)
        probs_low = probs.astype(jnp.bfloat16)
        dprobs = jnp.einsum(
            "qhd,kd->hqk", cot_block, seen_values, preferred_element_type=jnp.float32
        )
        deltas = jnp.sum(probs * dprobs, axis=2, keepdims=True)
        dscores = (probs * (dprobs - deltas)).astype(jnp.bfloat16)
        grad_block = (
            jnp.einsum("hqk,kd->qhd", dscores, seen_keys, preferred_element_type=jnp.float32)
            * scale_factor
        )
        query_blocks.append(grad_block.astype(jnp.bfloat16).reshape(block, local_heads * HEAD_SIZE))
        key_term = jnp.einsum(
            "hqk,qhd->kd", dscores, query_block, preferred_element_type=jnp.float32
        )
        value_term = jnp.einsum(
            "hqk,qhd->kd", probs_low, cot_block, preferred_element_type=jnp.float32
        )
        key_total = key_total.at[low_row:stop_row].add(key_term)
        value_total = value_total.at[low_row:stop_row].add(value_term)
    grad_heads = jnp.concatenate(query_blocks, axis=0)
    pair_grads = jnp.concatenate([key_total * scale_factor, value_total], axis=1).astype(
        jnp.bfloat16
    )
    grad_tokens, pair_slots = (
        lax.all_to_all(grad_heads[None, None], "seq", split_axis=2, concat_axis=3, tiled=True),
        lax.all_to_all(pair_grads[None, None], "seq", split_axis=2, concat_axis=3, tiled=True),
    )
    tok_rows = grad_tokens.shape[2]
    pair_sum = pair_slots.reshape(1, 1, tok_rows, HK, groups // HK, 2 * HEAD_SIZE).astype(
        jnp.float32
    )
    pair_tokens = (
        jnp.sum(pair_sum, axis=4).astype(jnp.bfloat16).reshape(1, 1, tok_rows, HK * 2 * HEAD_SIZE)
    )
    weight_term = contract_first(adapter_row_list, grad_heads)
    weight_share = lax.psum_scatter(
        weight_term.astype(jnp.bfloat16), "dp", scatter_dimension=0, tiled=True
    ).astype(jnp.float32)[None]
    input_grad = lax.psum_scatter(
        contract_last(grad_heads, local_adapter_part), "seq", scatter_dimension=0, tiled=True
    )
    input_grad = input_grad.astype(jnp.bfloat16)[None, None]
    return (grad_tokens, pair_tokens, input_grad, weight_share)


def solution(mesh):
    placed = (
        P("section", "dp", "seq", None),
        P("section", "dp", "seq", None),
        P("section", "dp", "seq", None),
        P("section", None, "seq"),
        P("section", "dp", "seq", None),
        P("section", "dp", None),
    )
    return jax.shard_map(
        per_device,
        mesh=mesh,
        in_specs=placed,
        out_specs=(
            P("section", "dp", "seq", None),
            P("section", "dp", "seq", None),
            P("section", "dp", "seq", None),
            P("section", "dp", "seq"),
        ),
        check_vma=False,
    )
```

profile of v0, /device:TPU:2, one launch (start us, length us, event | category | flops | bytes accessed | tf_op | source)
XLA Modules:
  0.0 609.5 jit_solution(15494971162059821550)
XLA Ops:
  7.2 5.0 copy.352
  12.7 22.4 %reduce.34 = bf16[4096,128]{1,0:T(8,128)(2,1)S(1)} reduce(bf16[4096,1,1,128]{3,2,1,0:T(2,128)(2,1)S(1)} %bitcast.553, bf16[]{:T(256)} %broadcast.641), dimensions={1,2}, to_apply=%bitcast.435.reduce_sub_computation | reduce | bytes 2097154
  36.3 17.8 %all-to-all-start = ((bf16[16,2,16384]{2,1,0:T(2,128)(2,1)}), bf16[16,2,16384]{2,1,0:T(2,128)(2,1)S(1)}, u32[]{:S(2)}, u32[]{:S(2)}) async-start(bf16[16,2,16384]{2,1,0:T(2,128)(2,1)} %reshape.1154), calls=%async_computation | async-start | bytes 2097152 | tf_op jit(solution)/shard_map/all_to_all | solution.py:39
  55.0 12.2 %collective-permute-done = bf16[1,1,128,4096]{3,2,1,0:T(8,128)(2,1)} collective-permute-done((bf16[1,1,128,4096]{3,2,1,0:T(8,128)(2,1)S(1)}, bf16[1,1,128,4096]{3,2,1,0:T(8,128)(2,1)}, u32[]{:S(2)}, u32[]{:S(2)}) %collective-permute-start) | collective-permute-done | bytes 1048608 | tf_op jit(solution)/shard_map/ppermute | solution.py:16
  67.2 5.0 copy.355
  72.2 23.4 %reduce.35 = bf16[4096,128]{1,0:T(8,128)(2,1)} reduce(bf16[4096,1,1,128]{3,2,1,0:T(2,128)(2,1)S(1)} %bitcast.554, bf16[]{:T(256)} %broadcast.641), dimensions={1,2}, to_apply=%bitcast.433.reduce_sub_computation | reduce | bytes 2097154
  97.8 19.2 %all-to-all-done = bf16[16,2,16384]{2,1,0:T(2,128)(2,1)S(1)} async-done(((bf16[16,2,16384]{2,1,0:T(2,128)(2,1)}), bf16[16,2,16384]{2,1,0:T(2,128)(2,1)S(1)}, u32[]{:S(2)}, u32[]{:S(2)}) %all-to-all-start) | async-done | bytes 1048608 | tf_op jit(solution)/shard_map/all_to_all | solution.py:39
  117.0 10.9 %all-to-all-start.1 = ((bf16[16,2,16384]{2,1,0:T(2,128)(2,1)}), bf16[16,2,16384]{2,1,0:T(2,128)(2,1)}, u32[]{:S(2)}, u32[]{:S(2)}) async-start(bf16[16,2,16384]{2,1,0:T(2,128)(2,1)} %reshape.1152), calls=%async_computation.1 | async-start | bytes 2097152 | tf_op jit(solution)/shard_map/all_to_all | solution.py:40
  128.0 137.2 %all_gather.7 = bf16[1,1,2048,64]{2,3,1,0:T(8,128)(2,1)S(1)} all-gather(bf16[1,1,128,64]{2,3,1,0:T(8,128)(2,1)S(1)} %copy-done.50), channel_id=1, replica_groups=mesh['section'=8,'seq'=16,'dp'=4] {'seq'}, dimensions={2}, use_global_device_ids=true | all-gather | bytes 278528 | tf_op jit(solution)/shard_map/all_gather | solution.py:41
  277.7 4.4 reshape.1153
  291.9 2.4 fusion.122
  301.5 2.4 fusion.124
  306.8 2.3 fusion.125
  311.8 2.3 fusion.126
  321.8 2.4 fusion.128
  342.4 4.6 copy.429
  347.0 11.6 %reduce.37 = bf16[2048,256]{1,0:T(8,128)(2,1)} reduce(bf16[2048,1,1,256]{3,2,1,0:T(2,128)(2,1)S(1)} %bitcast.557, bf16[]{:T(256)} %broadcast.641), dimensions={1,2}, to_apply=%bitcast.439.reduce_sub_computation | reduce | bytes 2097154
  360.8 8.6 %all-to-all-start.3 = ((bf16[16,2,16384]{2,1,0:T(2,128)(2,1)}), bf16[16,2,16384]{2,1,0:T(2,128)(2,1)}, u32[]{:S(2)}, u32[]{:S(2)}) async-start(bf16[16,2,16384]{2,1,0:T(2,128)(2,1)} %reshape.1158), calls=%async_computation.3 | async-start | bytes 2097152 | tf_op jit(solution)/shard_map/all_to_all | solution.py:104
  383.7 11.7 %copy.506 = bf16[1,1,2048,256]{3,1,0,2:T(2,128)(2,1)S(1)} copy(bf16[1,1,2048,256]{3,2,1,0:T(8,128)(2,1)S(1)} %bitcast.549) | data formatting | bytes 2097152 | tf_op jit(solution)/shard_map/broadcast_in_dim | solution.py:103
  395.4 11.6 %reduce.36 = bf16[2048,256]{1,0:T(8,128)(2,1)} reduce(bf16[2048,1,1,256]{3,2,1,0:T(2,128)(2,1)S(1)} %bitcast.558, bf16[]{:T(256)} %broadcast.641), dimensions={1,2}, to_apply=%bitcast.548.reduce_sub_computation | reduce | bytes 2097154
  409.2 14.4 %all-to-all-start.2 = ((bf16[16,2,16384]{2,1,0:T(2,128)(2,1)}), bf16[16,2,16384]{2,1,0:T(2,128)(2,1)S(1)}, u32[]{:S(2)}, u32[]{:S(2)}) async-start(bf16[16,2,16384]{2,1,0:T(2,128)(2,1)} %reshape.1156), calls=%async_computation.2 | async-start | bytes 2097152 | tf_op jit(solution)/shard_map/all_to_all | solution.py:103
  425.9 48.2 %reduce-scatter.5.cloned.1.call-done = bf16[16,256]{1,0:T(8,128)(2,1)} async-done(((bf16[64,256]{1,0:T(8,128)(2,1)}), bf16[16,256]{1,0:T(8,128)(2,1)}) %reduce-scatter.5.cloned.1.call-update) | async-done | bytes 8208 | tf_op jit(solution)/shard_map/reduce_scatter | solution.py:114
  475.4 114.7 %reduce-scatter.3.cloned.1.call-done = f32[128,64]{0,1:T(8,128)} async-done(((f32[2048,64]{0,1:T(8,128)}), f32[128,64]{0,1:T(8,128)}) %reduce-scatter.3.cloned.1.call-update) | async-done | bytes 32784 | tf_op jit(solution)/shard_map/reduce_scatter | solution.py:117
  591.5 4.3 reshape.1159
  (246 shorter events, 94.9 us)
Async XLA Ops:
  7.2 268.8 %copy-start = (bf16[1,64,256]{2,1,0:T(8,128)(2,1)S(1)}, bf16[1,64,256]{2,1,0:T(8,128)(2,1)}, u32[]{:S(2)}) copy-start(bf16[1,64,256]{2,1,0:T(8,128)(2,1)} %param.41) | copy-start | bytes 98308
  35.1 19.7 %copy-start.51 = (bf16[1,1,128,4096]{3,2,1,0:T(8,128)(2,1)S(1)}, bf16[1,1,128,4096]{3,2,1,0:T(8,128)(2,1)}, u32[]{:S(2)}) copy-start(bf16[1,1,128,4096]{3,2,1,0:T(8,128)(2,1)} %param.42) | copy-start | bytes 3145732
  36.3 80.8 %all-to-all-start = ((bf16[16,2,16384]{2,1,0:T(2,128)(2,1)}), bf16[16,2,16384]{2,1,0:T(2,128)(2,1)S(1)}, u32[]{:S(2)}, u32[]{:S(2)}) async-start(bf16[16,2,16384]{2,1,0:T(2,128)(2,1)} %reshape.1154), calls=%async_computation | async-start | bytes 2097152 | tf_op jit(solution)/shard_map/all_to_all | solution.py:39
  54.1 234.7 %all-gather.2.cloned.1.call-start = ((), (), s32[]{:S(2)}) async-start(), calls=%async_computation.6 | async-start | bytes 4456448 | tf_op jit(solution)/shard_map/all_gather | solution.py:42
  54.8 12.3 %collective-permute-start = (bf16[1,1,128,4096]{3,2,1,0:T(8,128)(2,1)S(1)}, bf16[1,1,128,4096]{3,2,1,0:T(8,128)(2,1)}, u32[]{:S(2)}, u32[]{:S(2)}) collective-permute-start(bf16[1,1,128,4096]{3,2,1,0:T(8,128)(2,1)S(1)} %copy-done.51), channel_id=1, source_target_pairs={{0,448},{64,0},{128,64},{192,128},{256,192},{320,256},{384,320},{4... | collective-permute-start | bytes 3145736 | tf_op jit(solution)/shard_map/ppermute | solution.py:16
  95.6 32.4 %copy-start.50 = (bf16[1,1,128,64]{2,3,1,0:T(8,128)(2,1)S(1)}, bf16[1,1,128,64]{2,3,1,0:T(8,128)(2,1)}, u32[]{:S(2)}) copy-start(bf16[1,1,128,64]{2,3,1,0:T(8,128)(2,1)} %param.40) | copy-start | bytes 49156
  95.6 169.7 %copy-start.49 = (s32[1,1,2048]{2,1,0:T(1,128)S(1)}, s32[1,1,2048]{2,1,0:T(1,128)}, u32[]{:S(2)}) copy-start(s32[1,1,2048]{2,1,0:T(1,128)} %param.43) | copy-start | bytes 24580
  117.0 160.7 %all-to-all-start.1 = ((bf16[16,2,16384]{2,1,0:T(2,128)(2,1)}), bf16[16,2,16384]{2,1,0:T(2,128)(2,1)}, u32[]{:S(2)}, u32[]{:S(2)}) async-start(bf16[16,2,16384]{2,1,0:T(2,128)(2,1)} %reshape.1152), calls=%async_computation.1 | async-start | bytes 2097152 | tf_op jit(solution)/shard_map/all_to_all | solution.py:40
  265.3 10.7 %copy-start.11 = (bf16[1,1,2048,64]{2,3,1,0:T(8,128)(2,1)}, bf16[1,1,2048,64]{2,3,1,0:T(8,128)(2,1)S(1)}, u32[]{:S(2)}) copy-start(bf16[1,1,2048,64]{2,3,1,0:T(8,128)(2,1)S(1)} %all_gather.7) | copy-start | bytes 786436
  277.7 12.3 %copy-start.29 = (bf16[256,256]{0,1:T(8,128)(2,1)}, bf16[256,256]{0,1:T(8,128)(2,1)S(1)}, u32[]{:S(2)}) copy-start(bf16[256,256]{0,1:T(8,128)(2,1)S(1)} %get-tuple-element.215) | copy-start | bytes 393220
  290.0 13.8 %copy-start.10 = (bf16[2048,256]{1,0:T(8,128)(2,1)}, bf16[2048,256]{1,0:T(8,128)(2,1)S(1)}, u32[]{:S(2)}) copy-start(bf16[2048,256]{1,0:T(8,128)(2,1)S(1)} %dynamic-slice_bitcast_fusion) | copy-start | bytes 3145732
  306.5 4.4 copy-start.1
  311.0 4.8 copy-start.3
  316.0 4.8 copy-start.5
  321.1 4.9 copy-start.7
  360.8 12.3 %copy-start.8 = (bf16[2,256,512]{1,2,0:T(8,128)(2,1)S(1)}, bf16[2,256,512]{1,2,0:T(8,128)(2,1)}, u32[]{:S(2)}) copy-start(bf16[2,256,512]{1,2,0:T(8,128)(2,1)} %copy-done.7) | copy-start | bytes 1572868
  360.8 15.1 %copy-start.6 = (bf16[2,256,512]{1,2,0:T(8,128)(2,1)S(1)}, bf16[2,256,512]{1,2,0:T(8,128)(2,1)}, u32[]{:S(2)}) copy-start(bf16[2,256,512]{1,2,0:T(8,128)(2,1)} %copy-done.5) | copy-start | bytes 1572868
  360.8 48.4 %all-to-all-start.3 = ((bf16[16,2,16384]{2,1,0:T(2,128)(2,1)}), bf16[16,2,16384]{2,1,0:T(2,128)(2,1)}, u32[]{:S(2)}, u32[]{:S(2)}) async-start(bf16[16,2,16384]{2,1,0:T(2,128)(2,1)} %reshape.1158), calls=%async_computation.3 | async-start | bytes 2097152 | tf_op jit(solution)/shard_map/all_to_all | solution.py:104
  369.4 7.9 %copy-start.4 = (bf16[2,256,512]{1,2,0:T(8,128)(2,1)S(1)}, bf16[2,256,512]{1,2,0:T(8,128)(2,1)}, u32[]{:S(2)}) copy-start(bf16[2,256,512]{1,2,0:T(8,128)(2,1)} %copy-done.3) | copy-start | bytes 1572868
  369.4 9.1 %copy-start.2 = (bf16[2,256,512]{1,2,0:T(8,128)(2,1)S(1)}, bf16[2,256,512]{1,2,0:T(8,128)(2,1)}, u32[]{:S(2)}) copy-start(bf16[2,256,512]{1,2,0:T(8,128)(2,1)} %copy-done.1) | copy-start | bytes 1572868
  407.0 16.6 %copy-start.12 = (bf16[1,1,2048,64]{2,3,1,0:T(8,128)(2,1)S(1)}, bf16[1,1,2048,64]{2,3,1,0:T(8,128)(2,1)}, u32[]{:S(2)}) copy-start(bf16[1,1,2048,64]{2,3,1,0:T(8,128)(2,1)} %copy-done.11) | copy-start | bytes 786436
  409.2 190.2 %all-to-all-start.2 = ((bf16[16,2,16384]{2,1,0:T(2,128)(2,1)}), bf16[16,2,16384]{2,1,0:T(2,128)(2,1)S(1)}, u32[]{:S(2)}, u32[]{:S(2)}) async-start(bf16[16,2,16384]{2,1,0:T(2,128)(2,1)} %reshape.1156), calls=%async_computation.2 | async-start | bytes 2097152 | tf_op jit(solution)/shard_map/all_to_all | solution.py:103
  423.6 50.5 %reduce-scatter.5.cloned.1.call-start = ((), (), s32[]{:S(2)}) async-start(), calls=%async_computation.8 | async-start | bytes 40960 | tf_op jit(solution)/shard_map/reduce_scatter | solution.py:114
  424.6 165.5 %reduce-scatter.3.cloned.1.call-start = ((), (), s32[]{:S(2)}) async-start(), calls=%async_computation.7 | async-start | bytes 557056 | tf_op jit(solution)/shard_map/reduce_scatter | solution.py:117
  (36 other events, 55.5 us)
Sparse Core Ops, SparseCore 0:
  57.9 175.9 all-gather.1
  427.8 46.2 reduce-scatter.4
  479.3 110.7 reduce-scatter.2
where the time goes:
time: 620 us; the launch traced here: 610 us
  waiting for transfers between devices  195 us (31%)
  blocking collectives  137 us (22%)
  other arithmetic  85.7 us (14%)
  local copies, waits for them, and re-layouts  66.9 us (11%)
  matrix products  57.3 us (9%)
  starting transfers between devices  51.9 us (8%)
  between operations  15.5 us (2%)
    all_gather x1, blocking collectives, per_device(): lax.all_gather(adapter_input, 'seq', axis=2, tiled=True)[0, 0]  137 us
    reduce_scatter x1, waiting for transfers between devices, per_device(): lax.psum_scatter(contract_last(grad_heads, local_adapter_part), 'seq', sc...  115 us
    unnamed x4, other arithmetic  69 us
    reduce_scatter x1, waiting for transfers between devices, per_device(): lax.psum_scatter(weight_term.astype(jnp.bfloat16), 'dp', scatter_dimensio...  48.2 us
    unnamed x127, local copies, waits for them, and re-layouts  31.3 us
    all_to_all x1, waiting for transfers between devices, per_device(): lax.all_to_all(frozen_queries, 'seq', split_axis=3, concat_axis=2, tiled=...  19.2 us
    all_to_all x1, starting transfers between devices, per_device(): lax.all_to_all(frozen_queries, 'seq', split_axis=3, concat_axis=2, tiled=...  17.8 us
    sub x8, matrix products, per_device(): shifted = jnp.exp(scores - jnp.max(scores, axis=2, keepdims=True))  16 us
  transfers between devices with their start and end apart: 8, of which 4 were waited for; matrix products, arithmetic and copies ran while one was open for 17% of the time, Pallas kernels for 0%

commit v1 on v0

v1 whole, which is shorter than its diff:
```python
import functools
import math

import jax
import jax.numpy as jnp
from jax import lax
from jax.experimental import pallas as pl
from jax.experimental.pallas import tpu as pltpu
from jax.sharding import PartitionSpec as P

HEAD = 128
ROWS = 128
HALF = ROWS // 2
PAIR = 2 * HEAD
WIDE = 8 * HEAD
RANK = 64
PART = RANK // 4
CHUNK = 2
SCALE = 1.0 / math.sqrt(HEAD)
LOW = -1e30
MESH = pl.DeviceIdType.MESH
BF16 = jnp.bfloat16
F32 = jnp.float32


def dot(left, right, left_dim, right_dim):
    return lax.dot_general(
        left, right, (((left_dim,), (right_dim,)), ((), ())), preferred_element_type=F32
    )


def kernel(
    q_hbm, kv_hbm, a_hbm, w_hbm, up_hbm, doc_ref,
    dq_hbm, dkv_hbm, da_ref, dw_ref,
    qf, cot, kvw, xs, wall, a_v, bias, own, dkvs, landed, ds, dso, kvo, dqv, da_acc,
    ws, wr, wz, wl, wh, wf, w_own,
    q_sem, kv_sem, a_sem, wl_sem, dq_sem, dkv_sem,
    cot_s, cot_r, az_s, az_r, ay_s, ay_r,
    n1_s, n1_r, n2_s, n2_r, fw_s, x1_s, x1_r, x2_s, x2_r,
    m1_s, m1_r, m2_s, m2_r, d1_s, d1_r, d2_s, d2_r,
    wy_s, wy_r, wl_s, wl_r, wh_s, wh_r,
):
    sec = lax.axis_index("section")
    p = lax.axis_index("seq")
    l = lax.axis_index("dp")
    y = lax.rem(p, 4)
    h = lax.div(p, 4)

    def mod4(v):
        return lax.rem(v + 8, 4)

    def at(h_, y_):
        return {"seq": h_ * 4 + y_}

    def remote(src, dst, s, r, where):
        return pltpu.make_async_remote_copy(
            src_ref=src, dst_ref=dst, send_sem=s, recv_sem=r,
            device_id=where, device_id_type=MESH,
        )

    def group(i):
        return mod4(h + i)

    def kv_cols(g):
        return pl.ds(pl.multiple_of(g * PAIR, PAIR), PAIR)

    def q_cols(g):
        return pl.ds(pl.multiple_of(g * WIDE, WIDE), WIDE)

    def load_q(i):
        return pltpu.make_async_copy(q_hbm.at[0, 0, :, q_cols(group(i))], qf.at[i], q_sem.at[i])

    def load_kv(i):
        return pltpu.make_async_copy(
            kv_hbm.at[0, 0, :, kv_cols(group(i))], kvw.at[i, pl.ds(2 * ROWS, ROWS)], kv_sem.at[i]
        )

    def load_a():
        return pltpu.make_async_copy(a_hbm.at[0, 0], a_v, a_sem)

    def load_w():
        return pltpu.make_async_copy(w_hbm.at[0], wall.at[p], wl_sem)

    def send_cot(i):
        return remote(
            up_hbm.at[0, 0, :, q_cols(group(i))], cot.at[i], cot_s.at[i], cot_r.at[i],
            {"section": lax.rem(sec + 7, 8)},
        )

    def send_az(i):
        return remote(
            w_hbm.at[0], wall.at[p], az_s.at[i - 1], az_r.at[i - 1], at(mod4(h - i), y)
        )

    def send_ay(i, d):
        shard = wall.at[group(i) * 4 + y]
        return remote(shard, shard, ay_s.at[i, d - 1], ay_r.at[i, d - 1], at(h, mod4(y + d)))

    def send_n1(i):
        return remote(
            kv_hbm.at[0, 0, :, kv_cols(group(i))], kvw.at[i, pl.ds(ROWS, ROWS)],
            n1_s.at[i], n1_r.at[i], at(h, mod4(y + 1)),
        )

    def send_n2(i):
        return remote(
            kv_hbm.at[0, 0, :, kv_cols(group(i))], kvw.at[i, pl.ds(0, ROWS)],
            n2_s.at[i], n2_r.at[i], at(h, mod4(y + 2)),
        )

    def send_fwd(i):
        return remote(
            kvw.at[i, pl.ds(ROWS, ROWS)], kvw.at[i, pl.ds(0, ROWS)],
            fw_s.at[i], n2_r.at[i], at(h, mod4(y + 1)),
        )

    def send_x1(j, first, where):
        return remote(
            kv_hbm.at[0, 0, pl.ds(first, HALF), kv_cols(group(j + 1))], xs.at[j],
            x1_s.at[j], x1_r.at[j], at(h, where),
        )

    def send_x2_own(j, first, row, src_y):
        return remote(
            kv_hbm.at[0, 0, pl.ds(first, HALF), kv_cols(group(j + 1))],
            kvw.at[j, pl.ds(row, HALF)], x2_s.at[j], x2_r.at[src_y, j], at(mod4(h + 1), 0),
        )

    def send_x2_staged(j, row, src_y):
        return remote(
            xs.at[j], kvw.at[j, pl.ds(row, HALF)], x2_s.at[j], x2_r.at[src_y, j],
            at(mod4(h + 1), 0),
        )

    def wait_x2(j, row, src_y):
        send_x2_staged(j, row, src_y).wait_recv()

    def send_m1(i):
        return remote(
            dkvs.at[i, pl.ds(ROWS, ROWS)], landed.at[i, pl.ds(0, ROWS)],
            m1_s.at[i], m1_r.at[i], at(h, mod4(y - 1)),
        )

    def send_m2(i):
        return remote(
            dkvs.at[i, pl.ds(0, ROWS)], landed.at[i, pl.ds(ROWS, ROWS)],
            m2_s.at[i], m2_r.at[i], at(h, mod4(y - 2)),
        )

    def send_d1(i, row, slot, k, where):
        return remote(
            dkvs.at[i, pl.ds(row, HALF)], ds.at[i, slot],
            d1_s.at[i, k], d1_r.at[i, slot], at(h, where),
        )

    def send_d2(i, src, row, k, where):
        return remote(
            src, landed.at[lax.rem(i + 1, 4), pl.ds(row, HALF)],
            d2_s.at[i], d2_r.at[lax.rem(i + 1, 4), k], at(mod4(h - 1), where),
        )

    def send_wy(i, d):
        to = mod4(y + d)
        return remote(ws.at[i, to], wr.at[i, d - 1], wy_s.at[i, d - 1], wy_r.at[i, d - 1], at(h, to))

    def send_wl(i, d):
        to = mod4(l + d)
        return remote(
            wz.at[i, pl.ds(pl.multiple_of(to * PART, PART), PART)], wl.at[i, d - 1],
            wl_s.at[i, d - 1], wl_r.at[i, d - 1], {"dp": to},
        )

    def send_wh(i):
        return remote(wh.at[i - 1], wf.at[i - 1], wh_s.at[i - 1], wh_r.at[i - 1], at(group(i), y))

    def store_dq(i):
        return pltpu.make_async_copy(dqv.at[i], dq_hbm.at[0, 0, :, q_cols(group(i))], dq_sem.at[i])

    def store_dkv(i):
        return pltpu.make_async_copy(
            kvo.at[i], dkv_hbm.at[0, 0, :, kv_cols(group(i))], dkv_sem.at[i]
        )

    low_h = h < 3
    high_h = h > 0

    load_w().start()
    load_a().start()
    for i in range(4):
        load_kv(i).start()
        load_q(i).start()

    bar = pltpu.get_barrier_semaphore()

    def greet(where):
        pl.semaphore_signal(bar, inc=1, device_id=where, device_id_type=MESH)

    greet({"section": lax.rem(sec + 7, 8)})
    greet({"section": lax.rem(sec + 1, 8)})
    for d in range(1, 4):
        greet(at(h, mod4(y + d)))
        greet(at(mod4(h + d), y))
        greet({"dp": mod4(l + d)})

    @pl.when((y == 0) & high_h)
    def _():
        for k in range(1, 4):
            greet(at(h - 1, k))

    @pl.when((y >= 1) & low_h)
    def _():
        greet(at(h + 1, 0))

    @pl.when((y == 1) & high_h)
    def _():
        greet(at(h - 1, 2))

    @pl.when((y == 2) & low_h)
    def _():
        greet(at(h + 1, 1))

    def docs(block):
        return doc_ref[0, :, pl.ds(pl.multiple_of(block * ROWS, ROWS), ROWS)].astype(F32)

    mine = jnp.broadcast_to(docs(p), (ROWS, ROWS))
    key_row = lax.broadcasted_iota(jnp.int32, (ROWS, ROWS), 0)
    query_col = lax.broadcasted_iota(jnp.int32, (ROWS, ROWS), 1)
    for k in range(3):
        back = 2 - k
        block = jnp.maximum(p - back, 0)
        theirs = jnp.broadcast_to(docs(block), (ROWS, ROWS)).T
        seen = theirs == mine
        if back == 0:
            seen = seen & (key_row <= query_col)
        else:
            seen = seen & (jnp.broadcast_to(p, (ROWS, ROWS)) >= back)
        bias[pl.ds(k * ROWS, ROWS), :] = jnp.where(seen, 0.0, LOW)

    @pl.when(p < 2)
    def _():
        kvw[:, pl.ds(0, ROWS), :] = jnp.zeros((4, ROWS, PAIR), BF16)

    @pl.when(p < 1)
    def _():
        kvw[:, pl.ds(ROWS, ROWS), :] = jnp.zeros((4, ROWS, PAIR), BF16)

    @pl.when((y == 3) | (p == 14))
    def _():
        landed[:, pl.ds(ROWS, ROWS), :] = jnp.zeros((4, ROWS, PAIR), BF16)

    @pl.when(p == 15)
    def _():
        landed[:, pl.ds(0, ROWS), :] = jnp.zeros((4, ROWS, PAIR), BF16)

    da_acc[...] = jnp.zeros((ROWS, RANK), F32)

    extra = (
        jnp.where((y == 0) & high_h, 3, 0)
        + jnp.where((y >= 1) & low_h, 1, 0)
        + jnp.where((y == 1) & high_h, 1, 0)
        + jnp.where((y == 2) & low_h, 1, 0)
    )
    pl.semaphore_wait(bar, 11 + extra)

    @pl.when((y == 2) & low_h)
    def _():
        for j in range(4):
            send_x1(j, HALF, 1).start()
        for j in range(4):
            send_x2_own(j, 0, 0, 2).start()

    @pl.when((y == 3) & low_h)
    def _():
        for j in range(4):
            send_x1(j, 0, 0).start()
        for j in range(4):
            send_x2_own(j, HALF, 192, 3).start()

    load_w().wait()
    for d in (1, 3, 2):
        send_ay(0, d).start()
    send_cot(0).start()
    for i in (1, 3, 2):
        send_az(i).start()

    for i in range(4):
        @pl.when(y < 3)
        def _():
            send_n1(i).start()

        @pl.when(y < 2)
        def _():
            send_n2(i).start()

    for i in range(1, 4):
        send_cot(i).start()

    @pl.when((y == 1) & low_h)
    def _():
        for j in range(4):
            send_x1(j, HALF, 1).wait_recv()
            send_x2_staged(j, 64, 1).start()

    @pl.when((y == 0) & low_h)
    def _():
        for j in range(4):
            send_x1(j, 0, 0).wait_recv()
            send_x2_staged(j, 128, 0).start()

    for i in (1, 3, 2):
        send_az(i).wait_recv()
        for d in (1, 3, 2):
            send_ay(i, d).start()

    load_a().wait()

    def work(i):
        g = group(i)
        for d in (1, 3, 2):
            send_ay(i, d).wait_recv()
        load_q(i).wait()
        load_kv(i).wait()

        @pl.when(y >= 1)
        def _():
            send_n1(i).wait_recv()

        @pl.when((y >= 2) | ((y == 1) & high_h))
        def _():
            send_n2(i).wait_recv()

        @pl.when((y == 0) & high_h)
        def _():
            wait_x2(i, 128, 0)
            wait_x2(i, 192, 3)
            send_fwd(i).start()
            wait_x2(i, 64, 1)
            wait_x2(i, 0, 2)

        send_cot(i).wait_recv()

        a_rows = a_v[...]
        w_g = jnp.concatenate([wall[g * 4 + k] for k in range(4)], axis=1)
        keys = kvw[i, :, :HEAD]
        values = kvw[i, :, HEAD:]
        d_key = jnp.zeros((3 * ROWS, HEAD), F32)
        d_value = jnp.zeros((3 * ROWS, HEAD), F32)
        da = da_acc[...]
        seen = bias[...]
        seen = jnp.concatenate([seen] * CHUNK, axis=1)
        for first in range(0, 8, CHUNK):
            cols = slice(first * HEAD, (first + CHUNK) * HEAD)
            w_cols = w_g[:, cols]
            queries = (qf[i, :, cols].astype(F32) + dot(a_rows, w_cols, 1, 0)).astype(BF16)
            cots = cot[i, :, cols]
            q_rows = jnp.concatenate(
                [queries[:, k * HEAD:(k + 1) * HEAD] for k in range(CHUNK)], axis=0
            )
            c_rows = jnp.concatenate(
                [cots[:, k * HEAD:(k + 1) * HEAD] for k in range(CHUNK)], axis=0
            )
            scores = dot(keys, q_rows, 1, 1) * (SCALE * math.log2(math.e)) + seen
            top = jnp.max(scores, axis=0, keepdims=True)
            raised = jnp.exp2(scores - top)
            probs = raised * (1.0 / jnp.sum(raised, axis=0, keepdims=True))
            dprobs = dot(values, c_rows, 1, 1)
            deltas = jnp.sum(probs * dprobs, axis=0, keepdims=True)
            dscores = (probs * (dprobs - deltas)).astype(BF16)
            d_value = d_value + dot(probs.astype(BF16), c_rows, 1, 0)
            d_key = d_key + dot(dscores, q_rows, 1, 0)
            dq_rows = (dot(dscores, keys, 0, 0) * SCALE).astype(BF16)
            dq = jnp.concatenate(
                [dq_rows[k * ROWS:(k + 1) * ROWS] for k in range(CHUNK)], axis=1
            )
            dqv[i, :, cols] = dq
            da = da + dot(dq, w_cols, 1, 1)
        da_acc[...] = da
        store_dq(i).start()
        grads = jnp.concatenate([d_key * SCALE, d_value], axis=1)
        own[i] = grads[2 * ROWS:]
        dkvs[i] = grads[:2 * ROWS].astype(BF16)

        @pl.when((y == 0) & high_h)
        def _():
            send_d1(i, 0, 0, 0, 2).start()
            send_d1(i, 64, 0, 1, 1).start()
            send_d1(i, 192, 0, 2, 3).start()

        @pl.when((y == 1) & high_h)
        def _():
            send_d1(i, 0, 0, 0, 0).start()
            send_d1(i, 64, 1, 1, 3).start()

        @pl.when(y >= 1)
        def _():
            send_m1(i).start()

        @pl.when(y >= 2)
        def _():
            send_m2(i).start()

        dw = dot(a_rows, dqv[i], 0, 0).astype(BF16)
        for k in range(4):
            ws[i, k] = dw[:, k * 256:(k + 1) * 256]
        for d in (1, 3, 2):
            send_wy(i, d).start()

    def second(i):
        @pl.when((y == 0) & high_h)
        def _():
            send_d1(i, 0, 0, 0, 0).wait_recv()
            dso[i] = (ds[i, 0].astype(F32) + dkvs[i, pl.ds(ROWS, HALF), :].astype(F32)).astype(BF16)
            send_d2(i, dso.at[i], 0, 0, 3).start()

        @pl.when((y == 3) & high_h)
        def _():
            send_d1(i, 0, 0, 0, 0).wait_recv()
            send_d1(i, 0, 1, 0, 0).wait_recv()
            dso[i] = (ds[i, 0].astype(F32) + ds[i, 1].astype(F32)).astype(BF16)
            send_d2(i, dso.at[i], 64, 1, 3).start()

        @pl.when((y == 1) & high_h)
        def _():
            send_d1(i, 0, 0, 0, 0).wait_recv()
            send_d2(i, ds.at[i, 0], 192, 1, 2).start()

        @pl.when((y == 2) & high_h)
        def _():
            send_d1(i, 0, 0, 0, 0).wait_recv()
            send_d2(i, ds.at[i, 0], 128, 0, 2).start()

        total = ws[i, y].astype(F32)
        for d in range(1, 4):
            send_wy(i, d).wait_recv()
            total = total + wr[i, d - 1].astype(F32)
        wz[i] = total.astype(BF16)
        for d in (1, 3, 2):
            send_wl(i, d).start()

    def third(i):
        total = wz[i, pl.ds(pl.multiple_of(l * PART, PART), PART), :].astype(F32)
        for d in range(1, 4):
            send_wl(i, d).wait_recv()
            total = total + wl[i, d - 1].astype(F32)

        @pl.when(i == 0)
        def _():
            w_own[...] = total

        @pl.when(i > 0)
        def _():
            wh[i - 1] = total.astype(BF16)
            send_wh(i).start()

    def round_(r, _):
        @pl.when(r < 4)
        def _():
            work(r)

        @pl.when((r >= 1) & (r < 5))
        def _():
            second(r - 1)

        @pl.when(r >= 2)
        def _():
            third(r - 2)

        return 0

    lax.fori_loop(0, 6, round_, 0)

    da_ref[0, 0] = da_acc[...].astype(BF16)

    def settle(i, _):
        @pl.when(y < 3)
        def _():
            send_m1(i).wait_recv()

        @pl.when(y < 2)
        def _():
            send_m2(i).wait_recv()

        @pl.when((y >= 2) & low_h)
        def _():
            send_d2(lax.rem(i + 3, 4), ds.at[i, 0], 0, 0, 2).wait_recv()
            send_d2(lax.rem(i + 3, 4), ds.at[i, 0], 0, 1, 2).wait_recv()

        total = (
            own[i]
            + landed[i, pl.ds(0, ROWS), :].astype(F32)
            + landed[i, pl.ds(ROWS, ROWS), :].astype(F32)
        )
        kvo[i] = total.astype(BF16)
        store_dkv(i).start()
        return 0

    lax.fori_loop(0, 4, settle, 0)
    total = w_own[...]
    for i in range(1, 4):
        send_wh(i).wait_recv()
        total = total + wf[i - 1].astype(F32)
    dw_ref[0] = total

    def drain(i, _):
        send_cot(i).wait_send()
        for d in range(1, 4):
            send_ay(i, d).wait_send()
            send_wy(i, d).wait_send()
            send_wl(i, d).wait_send()

        @pl.when(i > 0)
        def _():
            send_az(i).wait_send()
            send_wh(i).wait_send()

        @pl.when(y < 3)
        def _():
            send_n1(i).wait_send()

        @pl.when((y < 2))
        def _():
            send_n2(i).wait_send()

        @pl.when((y >= 2) & low_h)
        def _():
            send_x1(i, 0, 0).wait_send()

        @pl.when(low_h)
        def _():
            send_x2_staged(i, 0, 0).wait_send()

        @pl.when(y >= 1)
        def _():
            send_m1(i).wait_send()

        @pl.when(y >= 2)
        def _():
            send_m2(i).wait_send()

        @pl.when((y < 2) & high_h)
        def _():
            send_d1(i, 0, 0, 0, 0).wait_send()
            send_d1(i, 0, 0, 1, 0).wait_send()

        @pl.when((y == 0) & high_h)
        def _():
            send_d1(i, 0, 0, 2, 0).wait_send()
            send_fwd(i).wait_send()

        @pl.when(high_h)
        def _():
            send_d2(i, ds.at[i, 0], 0, 0, 2).wait_send()

        store_dq(i).wait()
        store_dkv(i).wait()
        return 0

    lax.fori_loop(0, 4, drain, 0)


def per_device(frozen_queries, key_value_pairs, adapter_input, adapter_up_matrix, upstream, document_index):
    any_ = pl.BlockSpec(memory_space=pl.ANY)
    vmem = pl.BlockSpec(memory_space=pltpu.VMEM)
    dma = pltpu.SemaphoreType.DMA
    scratch = [
        pltpu.VMEM((4, ROWS, WIDE), BF16),
        pltpu.VMEM((4, ROWS, WIDE), BF16),
        pltpu.VMEM((4, 3 * ROWS, PAIR), BF16),
        pltpu.VMEM((4, HALF, PAIR), BF16),
        pltpu.VMEM((16, RANK, 256), BF16),
        pltpu.VMEM((ROWS, RANK), BF16),
        pltpu.VMEM((3 * ROWS, ROWS), F32),
        pltpu.VMEM((4, ROWS, PAIR), F32),
        pltpu.VMEM((4, 2 * ROWS, PAIR), BF16),
        pltpu.VMEM((4, 2 * ROWS, PAIR), BF16),
        pltpu.VMEM((4, 2, HALF, PAIR), BF16),
        pltpu.VMEM((4, HALF, PAIR), BF16),
        pltpu.VMEM((4, ROWS, PAIR), BF16),
        pltpu.VMEM((4, ROWS, WIDE), BF16),
        pltpu.VMEM((ROWS, RANK), F32),
        pltpu.VMEM((4, 4, RANK, 256), BF16),
        pltpu.VMEM((4, 3, RANK, 256), BF16),
        pltpu.VMEM((4, RANK, 256), BF16),
        pltpu.VMEM((4, 3, PART, 256), BF16),
        pltpu.VMEM((3, PART, 256), BF16),
        pltpu.VMEM((3, PART, 256), BF16),
        pltpu.VMEM((PART, 256), F32),
        dma((4,)), dma((4,)), dma, dma, dma((4,)), dma((4,)),
        dma((4,)), dma((4,)), dma((3,)), dma((3,)), dma((4, 3)), dma((4, 3)),
        dma((4,)), dma((4,)), dma((4,)), dma((4,)), dma((4,)),
        dma((4,)), dma((4,)), dma((4,)), dma((4, 4)),
        dma((4,)), dma((4,)), dma((4,)), dma((4,)),
        dma((4, 3)), dma((4, 2)), dma((4,)), dma((4, 2)),
        dma((4, 3)), dma((4, 3)), dma((4, 3)), dma((4, 3)), dma((3,)), dma((3,)),
    ]
    return pl.pallas_call(
        kernel,
        out_shape=(
            jax.ShapeDtypeStruct((1, 1, ROWS, 4 * WIDE), BF16),
            jax.ShapeDtypeStruct((1, 1, ROWS, 4 * PAIR), BF16),
            jax.ShapeDtypeStruct((1, 1, ROWS, RANK), BF16),
            jax.ShapeDtypeStruct((1, PART, 256), F32),
        ),
        in_specs=[any_, any_, any_, any_, any_, vmem],
        out_specs=(any_, any_, vmem, vmem),
        scratch_shapes=scratch,
        compiler_params=pltpu.CompilerParams(
            collective_id=0, has_side_effects=True, vmem_limit_bytes=48 << 20
        ),
    )(frozen_queries, key_value_pairs, adapter_input, adapter_up_matrix, upstream, document_index)


def solution(mesh):
    placed = (
        P("section", "dp", "seq", None),
        P("section", "dp", "seq", None),
        P("section", "dp", "seq", None),
        P("section", None, "seq"),
        P("section", "dp", "seq", None),
        P("section", "dp", None),
    )
    return jax.shard_map(
        per_device,
        mesh=mesh,
        in_specs=placed,
        out_specs=(
            P("section", "dp", "seq", None),
            P("section", "dp", "seq", None),
            P("section", "dp", "seq", None),
            P("section", "dp", "seq"),
        ),
        check_vma=False,
    )
```

time: 620 us -> 82.2 us (0.13)
  the two profiles are of different devices: /device:TPU:2 before, /device:TPU:26 now
where the time goes in v1:
time: 82.2 us; the launch traced here: 81.9 us
  Pallas kernels  74 us (90%)
  local copies, waits for them, and re-layouts  7.21 us (9%)
    pallas_call x1, Pallas kernels, per_device(): pl.pallas_call(kernel, out_shape=(jax.ShapeDtypeStruct((1, 1, ROWS, 4 * W...  74 us
    unnamed x14, local copies, waits for them, and re-layouts  6.51 us

profile of v1, /device:TPU:26, one launch (start us, length us, event | category | flops | bytes accessed | tf_op | source)
XLA Modules:
  0.0 81.9 jit_solution(6253488980529428333)
XLA Ops:
  0.6 0.0 copy-start.4
  0.6 0.0 copy-start.3
  0.7 0.8 %copy.10.a_hbm = bf16[1,1,128,64]{3,2,1,0:T(8,128)(2,1)S(1)} copy(bf16[1,1,128,64]{2,3,1,0:T(8,128)(2,1)} %param.8) | data formatting | bytes 32768 | tf_op args[2]
  1.5 0.0 copy-done.4
  1.5 0.0 copy-done.3
  1.5 0.0 copy-start
  1.5 1.2 %copy-done = bf16[1,1,128,4096]{3,2,1,0:T(8,128)(2,1)S(1)} copy-done((bf16[1,1,128,4096]{3,2,1,0:T(8,128)(2,1)S(1)}, bf16[1,1,128,4096]{3,2,1,0:T(8,128)(2,1)}, u32[]{:S(2)}) %copy-start) | copy-done | bytes 1048600
  2.7 0.0 copy-start.1
  2.7 1.2 %copy-done.1 = bf16[1,1,128,4096]{3,2,1,0:T(8,128)(2,1)S(1)} copy-done((bf16[1,1,128,4096]{3,2,1,0:T(8,128)(2,1)S(1)}, bf16[1,1,128,4096]{3,2,1,0:T(8,128)(2,1)}, u32[]{:S(2)}) %copy-start.1) | copy-done | bytes 1048600
  4.0 0.0 copy-start.2
  4.0 0.9 %copy-done.2 = bf16[1,1,128,1024]{3,2,1,0:T(8,128)(2,1)S(1)} copy-done((bf16[1,1,128,1024]{3,2,1,0:T(8,128)(2,1)S(1)}, bf16[1,1,128,1024]{3,2,1,0:T(8,128)(2,1)}, u32[]{:S(2)}) %copy-start.2) | copy-done | bytes 262168
  4.9 74.0 %shard_map.93 = (bf16[1,1,128,4096]{3,2,1,0:T(8,128)(2,1)S(1)}, bf16[1,1,128,1024]{3,2,1,0:T(8,128)(2,1)S(1)}, bf16[1,1,128,64]{3,2,1,0:T(8,128)(2,1)S(1)}, f32[1,16,256]{2,1,0:T(8,128)S(1)}) custom-call(bf16[1,1,128,4096]{3,2,1,0:T(8,128)(2,1)S(1)} %copy-done, bf16[1,1,128,1024]{3,2,1,0:T(8,128)(2,1)S(1)} %copy-done.2, ...), custom_call_target="tpu_custom_call" | custom-call | tf_op jit(solution)/shard_map/pallas_call | solution.py:596
  78.9 0.7 copy.11
  79.6 1.0 %copy.15 = bf16[1,1,128,4096]{3,2,1,0:T(8,128)(2,1)} copy(bf16[1,1,128,4096]{3,2,1,0:T(8,128)(2,1)S(1)} %get-tuple-element.12) | data formatting | bytes 2097152
  80.6 0.7 copy.16
  81.3 0.6 copy.17
Async XLA Ops:
  0.6 0.9 %copy-start.4 = (s32[1,1,2048]{2,1,0:T(1,128)S(1)}, s32[1,1,2048]{2,1,0:T(1,128)}, u32[]{:S(2)}) copy-start(s32[1,1,2048]{2,1,0:T(1,128)} %doc_ref.1) | copy-start | bytes 24580
  0.6 0.9 %copy-start.3 = (bf16[1,64,256]{2,1,0:T(8,128)(2,1)S(1)}, bf16[1,64,256]{2,1,0:T(8,128)(2,1)}, u32[]{:S(2)}) copy-start(bf16[1,64,256]{2,1,0:T(8,128)(2,1)} %w_hbm.1) | copy-start | bytes 98308
  1.5 1.2 %copy-start = (bf16[1,1,128,4096]{3,2,1,0:T(8,128)(2,1)S(1)}, bf16[1,1,128,4096]{3,2,1,0:T(8,128)(2,1)}, u32[]{:S(2)}) copy-start(bf16[1,1,128,4096]{3,2,1,0:T(8,128)(2,1)} %q_hbm.1) | copy-start | bytes 3145732
  2.7 1.2 %copy-start.1 = (bf16[1,1,128,4096]{3,2,1,0:T(8,128)(2,1)S(1)}, bf16[1,1,128,4096]{3,2,1,0:T(8,128)(2,1)}, u32[]{:S(2)}) copy-start(bf16[1,1,128,4096]{3,2,1,0:T(8,128)(2,1)} %up_hbm.1) | copy-start | bytes 3145732
  4.0 0.9 %copy-start.2 = (bf16[1,1,128,1024]{3,2,1,0:T(8,128)(2,1)S(1)}, bf16[1,1,128,1024]{3,2,1,0:T(8,128)(2,1)}, u32[]{:S(2)}) copy-start(bf16[1,1,128,1024]{3,2,1,0:T(8,128)(2,1)} %kv_hbm.1) | copy-start | bytes 786436

commit v2 on v1

v2 whole, which is shorter than its diff:
```python
import functools
import math

import jax
import jax.numpy as jnp
from jax import lax
from jax.experimental import pallas as pl
from jax.experimental.pallas import tpu as pltpu
from jax.sharding import PartitionSpec as P

HEAD = 128
ROWS = 128
HALF = ROWS // 2
PAIR = 2 * HEAD
WIDE = 8 * HEAD
RANK = 64
PART = RANK // 4
CHUNK = 8
SCALE = 1.0 / math.sqrt(HEAD)
LOW = -1e30
MESH = pl.DeviceIdType.MESH
BF16 = jnp.bfloat16
F32 = jnp.float32


def dot(left, right, left_dim, right_dim):
    return lax.dot_general(
        left, right, (((left_dim,), (right_dim,)), ((), ())), preferred_element_type=F32
    )


def kernel(
    q_hbm, kv_hbm, a_hbm, w_hbm, up_hbm, doc_ref,
    dqv, kvo, da_ref, dw_ref,
    qf, cot, kvw, xs, wall, a_v, bias, own, dkvs, landed, ds, dso, da_acc,
    ws, wr, wz, wl, wh, wf, w_own,
    q_sem, kv_sem, a_sem, wl_sem,
    cot_s, cot_r, az_s, az_r, ay_s, ay_r,
    n1_s, n1_r, n2_s, n2_r, fw_s, x1_s, x1_r, x2_s, x2_r,
    m1_s, m1_r, m2_s, m2_r, d1_s, d1_r, d2_s, d2_r,
    wy_s, wy_r, wl_s, wl_r, wh_s, wh_r,
):
    sec = lax.axis_index("section")
    p = lax.axis_index("seq")
    l = lax.axis_index("dp")
    y = lax.rem(p, 4)
    h = lax.div(p, 4)

    def mod4(v):
        return lax.rem(v + 8, 4)

    def at(h_, y_):
        return {"seq": h_ * 4 + y_}

    def remote(src, dst, s, r, where):
        return pltpu.make_async_remote_copy(
            src_ref=src, dst_ref=dst, send_sem=s, recv_sem=r,
            device_id=where, device_id_type=MESH,
        )

    def group(i, at_h=None):
        at_h = h if at_h is None else at_h
        gray = jnp.where(i < 2, i, 5 - i)
        third = jnp.where(i == 0, 0, jnp.where(i == 1, 3, i - 1))
        return jnp.where(at_h == 1, i, jnp.where(at_h == 3, third, gray))

    def kv_cols(g):
        return pl.ds(pl.multiple_of(g * PAIR, PAIR), PAIR)

    def q_cols(g):
        return pl.ds(pl.multiple_of(g * WIDE, WIDE), WIDE)

    def load_q(g):
        return pltpu.make_async_copy(q_hbm.at[0, 0, :, q_cols(g)], qf.at[g], q_sem.at[g])

    def load_kv(g):
        return pltpu.make_async_copy(
            kv_hbm.at[0, 0, :, kv_cols(g)], kvw.at[g, pl.ds(2 * ROWS, ROWS)], kv_sem.at[g]
        )

    def load_a():
        return pltpu.make_async_copy(a_hbm.at[0, 0], a_v, a_sem)

    def load_w():
        return pltpu.make_async_copy(w_hbm.at[0], wall.at[p], wl_sem)

    def send_cot(g):
        return remote(
            up_hbm.at[0, 0, :, q_cols(g)], cot.at[g], cot_s.at[g], cot_r.at[g],
            {"section": lax.rem(sec + 7, 8)},
        )

    def send_az(shard, slot, there, to):
        src = wall.at[shard * 4 + y]
        return remote(src, src, az_s.at[slot], az_r.at[there], at(to, y))

    def send_az_up():
        return send_az(h, 0, 2, mod4(h + 1))

    def send_az_down():
        return send_az(h, 1, 0, mod4(h - 1))

    def send_az_relay():
        return send_az(mod4(h + 1), 2, 1, mod4(h - 1))

    def wait_az(away):
        send_az(h, 0, away - 1, mod4(h + 1)).wait_recv()

    def send_ay(g, d):
        shard = wall.at[g * 4 + y]
        return remote(shard, shard, ay_s.at[g, d - 1], ay_r.at[g, d - 1], at(h, mod4(y + d)))

    def mine(g, first, rows):
        return kvw.at[g, pl.ds(2 * ROWS + first, rows)]

    def send_n1(g):
        return remote(
            mine(g, 0, ROWS), kvw.at[g, pl.ds(ROWS, ROWS)],
            n1_s.at[g], n1_r.at[g], at(h, mod4(y + 1)),
        )

    def send_n2(g):
        return remote(
            mine(g, 0, ROWS), kvw.at[g, pl.ds(0, ROWS)],
            n2_s.at[g], n2_r.at[g], at(h, mod4(y + 2)),
        )

    def send_fwd(g):
        return remote(
            kvw.at[g, pl.ds(ROWS, ROWS)], kvw.at[g, pl.ds(0, ROWS)],
            fw_s.at[g], n2_r.at[g], at(h, mod4(y + 1)),
        )

    def send_x1(g, first, where):
        return remote(
            mine(g, first, HALF), xs.at[g], x1_s.at[g], x1_r.at[g], at(h, where)
        )

    def send_x2_own(g, first, row, src_y):
        return remote(
            mine(g, first, HALF), kvw.at[g, pl.ds(row, HALF)],
            x2_s.at[g], x2_r.at[src_y, g], at(mod4(h + 1), 0),
        )

    def send_x2_staged(g, row, src_y):
        return remote(
            xs.at[g], kvw.at[g, pl.ds(row, HALF)], x2_s.at[g], x2_r.at[src_y, g],
            at(mod4(h + 1), 0),
        )

    def wait_x2(g, row, src_y):
        send_x2_staged(g, row, src_y).wait_recv()

    def send_m1(g):
        return remote(
            dkvs.at[g, pl.ds(ROWS, ROWS)], landed.at[g, pl.ds(0, ROWS)],
            m1_s.at[g], m1_r.at[g], at(h, mod4(y - 1)),
        )

    def send_m2(g):
        return remote(
            dkvs.at[g, pl.ds(0, ROWS)], landed.at[g, pl.ds(ROWS, ROWS)],
            m2_s.at[g], m2_r.at[g], at(h, mod4(y - 2)),
        )

    def send_d1(g, row, slot, k, where):
        return remote(
            dkvs.at[g, pl.ds(row, HALF)], ds.at[g, slot],
            d1_s.at[g, k], d1_r.at[g, slot], at(h, where),
        )

    def send_d2(g, src, row, k, where):
        return remote(
            src, landed.at[g, pl.ds(row, HALF)],
            d2_s.at[g], d2_r.at[g, k], at(mod4(h - 1), where),
        )

    def send_wy(g, d):
        to = mod4(y + d)
        return remote(ws.at[g, to], wr.at[g, d - 1], wy_s.at[g, d - 1], wy_r.at[g, d - 1], at(h, to))

    def send_wl(g, d):
        to = mod4(l + d)
        return remote(
            wz.at[g, pl.ds(pl.multiple_of(to * PART, PART), PART)], wl.at[g, d - 1],
            wl_s.at[g, d - 1], wl_r.at[g, d - 1], {"dp": to},
        )

    def send_wh(g):
        slot = mod4(h - g + 3)
        return remote(wh.at[g], wf.at[slot], wh_s.at[g], wh_r.at[slot], at(g, y))

    def wait_wh(slot):
        remote(wh.at[0], wf.at[slot], wh_s.at[0], wh_r.at[slot], at(mod4(h + 1), y)).wait_recv()

    low_h = h < 3
    high_h = h > 0

    load_w().start()
    for g in range(4):
        load_kv(g).start()
    load_a().start()
    for g in range(4):
        load_q(g).start()

    bar = pltpu.get_barrier_semaphore()

    def greet(where):
        pl.semaphore_signal(bar, inc=1, device_id=where, device_id_type=MESH)

    greet({"section": lax.rem(sec + 7, 8)})
    greet({"section": lax.rem(sec + 1, 8)})
    greet(at(mod4(h + 1), y))
    greet(at(mod4(h - 1), y))
    for d in range(1, 4):
        greet(at(h, mod4(y + d)))
        greet({"dp": mod4(l + d)})

    @pl.when((y == 0) & high_h)
    def _():
        for k in range(1, 4):
            greet(at(h - 1, k))

    @pl.when((y >= 1) & low_h)
    def _():
        greet(at(h + 1, 0))

    @pl.when((y == 1) & high_h)
    def _():
        greet(at(h - 1, 2))

    @pl.when((y == 2) & low_h)
    def _():
        greet(at(h + 1, 1))

    def docs(block):
        return doc_ref[0, :, pl.ds(pl.multiple_of(block * ROWS, ROWS), ROWS)].astype(F32)

    my_docs = jnp.broadcast_to(docs(p), (ROWS, ROWS))
    key_row = lax.broadcasted_iota(jnp.int32, (ROWS, ROWS), 0)
    query_col = lax.broadcasted_iota(jnp.int32, (ROWS, ROWS), 1)
    for k in range(3):
        back = 2 - k
        block = jnp.maximum(p - back, 0)
        theirs = jnp.broadcast_to(docs(block), (ROWS, ROWS)).T
        seen = theirs == my_docs
        if back == 0:
            seen = seen & (key_row <= query_col)
        else:
            seen = seen & (jnp.broadcast_to(p, (ROWS, ROWS)) >= back)
        bias[pl.ds(k * ROWS, ROWS), :] = jnp.where(seen, 0.0, LOW)

    @pl.when(p < 2)
    def _():
        kvw[:, pl.ds(0, ROWS), :] = jnp.zeros((4, ROWS, PAIR), BF16)

    @pl.when(p < 1)
    def _():
        kvw[:, pl.ds(ROWS, ROWS), :] = jnp.zeros((4, ROWS, PAIR), BF16)

    @pl.when((y == 3) | (p == 14))
    def _():
        landed[:, pl.ds(ROWS, ROWS), :] = jnp.zeros((4, ROWS, PAIR), BF16)

    @pl.when(p == 15)
    def _():
        landed[:, pl.ds(0, ROWS), :] = jnp.zeros((4, ROWS, PAIR), BF16)

    da_acc[...] = jnp.zeros((RANK, ROWS), F32)

    extra = (
        jnp.where((y == 0) & high_h, 3, 0)
        + jnp.where((y >= 1) & low_h, 1, 0)
        + jnp.where((y == 1) & high_h, 1, 0)
        + jnp.where((y == 2) & low_h, 1, 0)
    )
    pl.semaphore_wait(bar, 10 + extra)

    for g in range(4):
        load_kv(g).wait()

    @pl.when((y == 2) & low_h)
    def _():
        for j in range(4):
            send_x1(group(j, h + 1), HALF, 1).start()
        for j in range(4):
            send_x2_own(group(j, h + 1), 0, 0, 2).start()

    @pl.when((y == 3) & low_h)
    def _():
        for j in range(4):
            send_x1(group(j, h + 1), 0, 0).start()
        for j in range(4):
            send_x2_own(group(j, h + 1), HALF, 192, 3).start()

    load_w().wait()
    for d in (1, 3, 2):
        send_ay(h, d).start()
    send_az_down().start()
    send_cot(group(0)).start()
    send_az_up().start()

    for i in range(4):
        g = group(i)
        if i > 0:
            send_cot(g).start()

        @pl.when(y < 3)
        def _():
            send_n1(g).start()

        @pl.when(y < 2)
        def _():
            send_n2(g).start()

    @pl.when((y == 1) & low_h)
    def _():
        for j in range(4):
            g = group(j, h + 1)
            send_x1(g, HALF, 1).wait_recv()
            send_x2_staged(g, 64, 1).start()

    @pl.when((y == 0) & low_h)
    def _():
        for j in range(4):
            g = group(j, h + 1)
            send_x1(g, 0, 0).wait_recv()
            send_x2_staged(g, 128, 0).start()

    def pass_shard(g):
        away = mod4(g - h)

        @pl.when(away > 0)
        def _():
            wait_az(away)

            @pl.when(away == 1)
            def _():
                send_az_relay().start()

            for d in (1, 3, 2):
                send_ay(g, d).start()

    pass_shard(group(0))
    load_a().wait()

    def work(r):
        i = group(r)
        g = i
        load_q(i).wait()

        @pl.when((y == 0) & high_h)
        def _():
            wait_x2(i, 128, 0)
            wait_x2(i, 192, 3)
            send_fwd(i).start()
            wait_x2(i, 64, 1)
            wait_x2(i, 0, 2)

        @pl.when(y >= 1)
        def _():
            send_n1(i).wait_recv()

        @pl.when((y >= 2) | ((y == 1) & high_h))
        def _():
            send_n2(i).wait_recv()

        send_cot(i).wait_recv()

        @pl.when(r < 3)
        def _():
            pass_shard(group(jnp.minimum(r + 1, 3)))

        for d in (1, 3, 2):
            send_ay(i, d).wait_recv()

        a_cols = a_v[...]
        w_g = jnp.concatenate([wall[g * 4 + k] for k in range(4)], axis=1)
        keys = kvw[i, :, :HEAD]
        values = kvw[i, :, HEAD:]
        d_key = jnp.zeros((3 * ROWS, HEAD), F32)
        d_value = jnp.zeros((3 * ROWS, HEAD), F32)
        da = da_acc[...]
        seen = bias[...]
        seen = jnp.concatenate([seen] * CHUNK, axis=1)
        for first in range(0, 8, CHUNK):
            cols = slice(first * HEAD, (first + CHUNK) * HEAD)
            w_cols = w_g[:, cols]
            queries = (qf[i, :, cols].astype(F32) + dot(a_cols, w_cols, 0, 0)).astype(BF16)
            cots = cot[i, :, cols]
            q_rows = jnp.concatenate(
                [queries[:, k * HEAD:(k + 1) * HEAD] for k in range(CHUNK)], axis=0
            )
            c_rows = jnp.concatenate(
                [cots[:, k * HEAD:(k + 1) * HEAD] for k in range(CHUNK)], axis=0
            )
            scores = dot(keys, q_rows, 1, 1) * (SCALE * math.log2(math.e)) + seen
            top = jnp.max(scores, axis=0, keepdims=True)
            raised = jnp.exp2(scores - top)
            probs = raised * (1.0 / jnp.sum(raised, axis=0, keepdims=True))
            dprobs = dot(values, c_rows, 1, 1)
            deltas = jnp.sum(probs * dprobs, axis=0, keepdims=True)
            dscores = (probs * (dprobs - deltas)).astype(BF16)
            d_value = d_value + dot(probs.astype(BF16), c_rows, 1, 0)
            d_key = d_key + dot(dscores, q_rows, 1, 0)
            dq_rows = (dot(dscores, keys, 0, 0) * SCALE).astype(BF16)
            dq = jnp.concatenate(
                [dq_rows[k * ROWS:(k + 1) * ROWS] for k in range(CHUNK)], axis=1
            )
            dqv[i, :, cols] = dq
            da = da + dot(w_cols, dq, 1, 1)
        da_acc[...] = da
        grads = jnp.concatenate([d_key * SCALE, d_value], axis=1)
        own[i] = grads[2 * ROWS:]
        dkvs[i] = grads[:2 * ROWS].astype(BF16)

        @pl.when((y == 0) & high_h)
        def _():
            send_d1(i, 0, 0, 0, 2).start()
            send_d1(i, 64, 0, 1, 1).start()
            send_d1(i, 192, 0, 2, 3).start()

        @pl.when((y == 1) & high_h)
        def _():
            send_d1(i, 0, 0, 0, 0).start()
            send_d1(i, 64, 1, 1, 3).start()

        @pl.when(y >= 1)
        def _():
            send_m1(i).start()

        @pl.when(y >= 2)
        def _():
            send_m2(i).start()

        dw = dot(a_cols, dqv[i], 1, 0).astype(BF16)
        for k in range(4):
            ws[i, k] = dw[:, k * 256:(k + 1) * 256]
        for d in (1, 3, 2):
            send_wy(i, d).start()

    def second(r):
        i = group(r)

        @pl.when((y == 0) & high_h)
        def _():
            send_d1(i, 0, 0, 0, 0).wait_recv()
            dso[i] = (ds[i, 0].astype(F32) + dkvs[i, pl.ds(ROWS, HALF), :].astype(F32)).astype(BF16)
            send_d2(i, dso.at[i], 0, 0, 3).start()

        @pl.when((y == 3) & high_h)
        def _():
            send_d1(i, 0, 0, 0, 0).wait_recv()
            send_d1(i, 0, 1, 0, 0).wait_recv()
            dso[i] = (ds[i, 0].astype(F32) + ds[i, 1].astype(F32)).astype(BF16)
            send_d2(i, dso.at[i], 64, 1, 3).start()

        @pl.when((y == 1) & high_h)
        def _():
            send_d1(i, 0, 0, 0, 0).wait_recv()
            send_d2(i, ds.at[i, 0], 192, 1, 2).start()

        @pl.when((y == 2) & high_h)
        def _():
            send_d1(i, 0, 0, 0, 0).wait_recv()
            send_d2(i, ds.at[i, 0], 128, 0, 2).start()

        total = ws[i, y].astype(F32)
        for d in range(1, 4):
            send_wy(i, d).wait_recv()
            total = total + wr[i, d - 1].astype(F32)
        wz[i] = total.astype(BF16)
        for d in (1, 3, 2):
            send_wl(i, d).start()

    def third(r):
        i = group(r)
        total = wz[i, pl.ds(pl.multiple_of(l * PART, PART), PART), :].astype(F32)
        for d in range(1, 4):
            send_wl(i, d).wait_recv()
            total = total + wl[i, d - 1].astype(F32)

        @pl.when(i == h)
        def _():
            w_own[...] = total

        @pl.when(i != h)
        def _():
            wh[i] = total.astype(BF16)
            send_wh(i).start()

    def round_(r, _):
        @pl.when(r < 4)
        def _():
            work(r)

        @pl.when((r >= 1) & (r < 5))
        def _():
            second(r - 1)

        @pl.when(r >= 2)
        def _():
            third(r - 2)

        return 0

    lax.fori_loop(0, 6, round_, 0)

    da_ref[...] = da_acc[...].astype(BF16)

    def settle(r, _):
        g = group(r)

        @pl.when(y < 3)
        def _():
            send_m1(g).wait_recv()

        @pl.when(y < 2)
        def _():
            send_m2(g).wait_recv()

        @pl.when((y >= 2) & low_h)
        def _():
            send_d2(g, ds.at[g, 0], 0, 0, 2).wait_recv()
            send_d2(g, ds.at[g, 0], 0, 1, 2).wait_recv()

        total = (
            own[g]
            + landed[g, pl.ds(0, ROWS), :].astype(F32)
            + landed[g, pl.ds(ROWS, ROWS), :].astype(F32)
        )
        kvo[g] = total.astype(BF16)
        return 0

    lax.fori_loop(0, 4, settle, 0)
    total = w_own[...]
    for k in range(3):
        wait_wh(k)
        total = total + wf[k].astype(F32)
    dw_ref[...] = total

    send_az_up().wait_send()
    send_az_down().wait_send()
    send_az_relay().wait_send()

    def drain(g, _):
        send_cot(g).wait_send()
        for d in range(1, 4):
            send_ay(g, d).wait_send()
            send_wy(g, d).wait_send()
            send_wl(g, d).wait_send()

        @pl.when(g != h)
        def _():
            send_wh(g).wait_send()

        @pl.when(y < 3)
        def _():
            send_n1(g).wait_send()

        @pl.when(y < 2)
        def _():
            send_n2(g).wait_send()

        @pl.when((y >= 2) & low_h)
        def _():
            send_x1(g, 0, 0).wait_send()

        @pl.when(low_h)
        def _():
            send_x2_staged(g, 0, 0).wait_send()

        @pl.when(y >= 1)
        def _():
            send_m1(g).wait_send()

        @pl.when(y >= 2)
        def _():
            send_m2(g).wait_send()

        @pl.when((y < 2) & high_h)
        def _():
            send_d1(g, 0, 0, 0, 0).wait_send()
            send_d1(g, 0, 0, 1, 0).wait_send()

        @pl.when((y == 0) & high_h)
        def _():
            send_d1(g, 0, 0, 2, 0).wait_send()
            send_fwd(g).wait_send()

        @pl.when(high_h)
        def _():
            send_d2(g, ds.at[g, 0], 0, 0, 2).wait_send()

        return 0

    lax.fori_loop(0, 4, drain, 0)


def finish(dq_ref, dkv_ref, da_ref, dw_ref, dq_hbm, dkv_hbm, da_hbm, dw_hbm, sems):
    copies = [
        (dq_ref.at[g], dq_hbm.at[0, 0, :, pl.ds(g * WIDE, WIDE)]) for g in range(4)
    ] + [
        (dkv_ref.at[g], dkv_hbm.at[0, 0, :, pl.ds(g * PAIR, PAIR)]) for g in range(4)
    ] + [(da_ref, da_hbm.at[0, 0]), (dw_ref, dw_hbm.at[0])]
    copies = [
        pltpu.make_async_copy(src, dst, sems.at[k]) for k, (src, dst) in enumerate(copies)
    ]
    for copy in copies:
        copy.start()
    for copy in copies:
        copy.wait()


def per_device(frozen_queries, key_value_pairs, adapter_input, adapter_up_matrix, upstream, document_index):
    hbm = pl.BlockSpec(memory_space=pltpu.HBM)
    vmem = pl.BlockSpec(memory_space=pltpu.VMEM)
    dma = pltpu.SemaphoreType.DMA
    scratch = [
        pltpu.VMEM((4, ROWS, WIDE), BF16),
        pltpu.VMEM((4, ROWS, WIDE), BF16),
        pltpu.VMEM((4, 3 * ROWS, PAIR), BF16),
        pltpu.VMEM((4, HALF, PAIR), BF16),
        pltpu.VMEM((16, RANK, 256), BF16),
        pltpu.VMEM((RANK, ROWS), BF16),
        pltpu.VMEM((3 * ROWS, ROWS), F32),
        pltpu.VMEM((4, ROWS, PAIR), F32),
        pltpu.VMEM((4, 2 * ROWS, PAIR), BF16),
        pltpu.VMEM((4, 2 * ROWS, PAIR), BF16),
        pltpu.VMEM((4, 2, HALF, PAIR), BF16),
        pltpu.VMEM((4, HALF, PAIR), BF16),
        pltpu.VMEM((RANK, ROWS), F32),
        pltpu.VMEM((4, 4, RANK, 256), BF16),
        pltpu.VMEM((4, 3, RANK, 256), BF16),
        pltpu.VMEM((4, RANK, 256), BF16),
        pltpu.VMEM((4, 3, PART, 256), BF16),
        pltpu.VMEM((4, PART, 256), BF16),
        pltpu.VMEM((3, PART, 256), BF16),
        pltpu.VMEM((PART, 256), F32),
        dma((4,)), dma((4,)), dma, dma,
        dma((4,)), dma((4,)), dma((3,)), dma((3,)), dma((4, 3)), dma((4, 3)),
        dma((4,)), dma((4,)), dma((4,)), dma((4,)), dma((4,)),
        dma((4,)), dma((4,)), dma((4,)), dma((4, 4)),
        dma((4,)), dma((4,)), dma((4,)), dma((4,)),
        dma((4, 3)), dma((4, 2)), dma((4,)), dma((4, 2)),
        dma((4, 3)), dma((4, 3)), dma((4, 3)), dma((4, 3)), dma((4,)), dma((3,)),
    ]
    results = pl.pallas_call(
        kernel,
        out_shape=(
            jax.ShapeDtypeStruct((4, ROWS, WIDE), BF16),
            jax.ShapeDtypeStruct((4, ROWS, PAIR), BF16),
            jax.ShapeDtypeStruct((RANK, ROWS), BF16),
            jax.ShapeDtypeStruct((PART, 256), F32),
        ),
        in_specs=[hbm, hbm, hbm, hbm, hbm, vmem],
        out_specs=(vmem,) * 4,
        scratch_shapes=scratch,
        compiler_params=pltpu.CompilerParams(
            collective_id=0, has_side_effects=True, vmem_limit_bytes=62 << 20
        ),
    )(
        frozen_queries, key_value_pairs, jnp.swapaxes(adapter_input, 2, 3),
        adapter_up_matrix, upstream, document_index,
    )
    dq, dkv, da, dw = pl.pallas_call(
        finish,
        out_shape=(
            jax.ShapeDtypeStruct((1, 1, ROWS, 4 * WIDE), BF16),
            jax.ShapeDtypeStruct((1, 1, ROWS, 4 * PAIR), BF16),
            jax.ShapeDtypeStruct((1, 1, RANK, ROWS), BF16),
            jax.ShapeDtypeStruct((1, PART, 256), F32),
        ),
        in_specs=[vmem] * 4,
        out_specs=(hbm,) * 4,
        scratch_shapes=[dma((10,))],
        compiler_params=pltpu.CompilerParams(vmem_limit_bytes=62 << 20),
    )(*results)
    return dq, dkv, jnp.swapaxes(da, 2, 3), dw


def solution(mesh):
    placed = (
        P("section", "dp", "seq", None),
        P("section", "dp", "seq", None),
        P("section", "dp", "seq", None),
        P("section", None, "seq"),
        P("section", "dp", "seq", None),
        P("section", "dp", None),
    )
    return jax.shard_map(
        per_device,
        mesh=mesh,
        in_specs=placed,
        out_specs=(
            P("section", "dp", "seq", None),
            P("section", "dp", "seq", None),
            P("section", "dp", "seq", None),
            P("section", "dp", "seq"),
        ),
        check_vma=False,
    )
```

time: 82.2 us -> 70.9 us (0.86)
  the two profiles are of different devices: /device:TPU:26 before, /device:TPU:12 now
where the time goes in v2:
time: 70.9 us; the launch traced here: 70.7 us
  Pallas kernels  70.1 us (99%)
    pallas_call x1, Pallas kernels, per_device(): pl.pallas_call(kernel, out_shape=(jax.ShapeDtypeStruct((4, ROWS, WIDE), B...  67.6 us
    pallas_call x1, Pallas kernels, per_device(): pl.pallas_call(finish, out_shape=(jax.ShapeDtypeStruct((1, 1, ROWS, 4 * W...  2.45 us

profile of v2, /device:TPU:12, one launch (start us, length us, event | category | flops | bytes accessed | tf_op | source)
XLA Modules:
  0.0 70.7 jit_solution(6051837096023675355)
XLA Ops:
  0.6 67.6 %shard_map.93 = (bf16[4,128,1024]{2,1,0:T(8,128)(2,1)}, bf16[4,128,256]{2,1,0:T(8,128)(2,1)}, bf16[64,128]{1,0:T(8,128)(2,1)}, f32[16,256]{1,0:T(8,128)}) custom-call(bf16[1,1,128,4096]{3,2,1,0:T(8,128)(2,1)} %q_hbm.1, bf16[1,1,128,1024]{3,2,1,0:T(8,128)(2,1)} %kv_hbm.1, bf16[1,1,64,128]{3,2,1,0:T(8,128)(2,1)} %bitcast.2, bf16[1,64,256]{2,1,0:T(8,128)(2,1)} %w_hbm.1, ...), custom_call_target="tpu_custom_call" | custom-call | tf_op jit(solution)/shard_map/pallas_call | solution.py:648
  68.2 2.4 %shard_map.94 = (bf16[1,1,128,4096]{3,2,1,0:T(8,128)(2,1)}, bf16[1,1,128,1024]{3,2,1,0:T(8,128)(2,1)}, bf16[1,1,64,128]{3,2,1,0:T(8,128)(2,1)}, f32[1,16,256]{2,1,0:T(8,128)}) custom-call(bf16[4,128,1024]{2,1,0:T(8,128)(2,1)} %get-tuple-element.12.dq_ref, bf16[4,128,256]{2,1,0:T(8,128)(2,1)} %get-tuple-element.13.dkv_ref, ...), custom_call_target="tpu_custom_call" | custom-call | tf_op jit(solution)/shard_map/pallas_call | solution.py:666

commit v3 on v2

--- a/solution.py
+++ b/solution.py
@@ -15,7 +15,6 @@
 WIDE = 8 * HEAD
 RANK = 64
 PART = RANK // 4
-CHUNK = 8
 SCALE = 1.0 / math.sqrt(HEAD)
 LOW = -1e30
 MESH = pl.DeviceIdType.MESH
@@ -33,12 +32,12 @@
     q_hbm, kv_hbm, a_hbm, w_hbm, up_hbm, doc_ref,
     dqv, kvo, da_ref, dw_ref,
     qf, cot, kvw, xs, wall, a_v, bias, own, dkvs, landed, ds, dso, da_acc,
-    ws, wr, wz, wl, wh, wf, w_own,
+    ws, wr, wz, wf,
     q_sem, kv_sem, a_sem, wl_sem,
     cot_s, cot_r, az_s, az_r, ay_s, ay_r,
     n1_s, n1_r, n2_s, n2_r, fw_s, x1_s, x1_r, x2_s, x2_r,
     m1_s, m1_r, m2_s, m2_r, d1_s, d1_r, d2_s, d2_r,
-    wy_s, wy_r, wl_s, wl_r, wh_s, wh_r,
+    wy_s, wy_r, wz_s, wz_r, far_sem,
 ):
     sec = lax.axis_index("section")
     p = lax.axis_index("seq")
@@ -60,9 +59,12 @@
 
     def group(i, at_h=None):
         at_h = h if at_h is None else at_h
-        gray = jnp.where(i < 2, i, 5 - i)
-        third = jnp.where(i == 0, 0, jnp.where(i == 1, 3, i - 1))
-        return jnp.where(at_h == 1, i, jnp.where(at_h == 3, third, gray))
+        zero = jnp.where(i < 2, i, 5 - i)
+        two = i + 1 - 2 * lax.rem(i, 2)
+        three = jnp.where(i == 0, 0, jnp.where(i == 1, 3, i - 1))
+        return jnp.where(
+            at_h == 0, zero, jnp.where(at_h == 1, i, jnp.where(at_h == 2, two, three))
+        )
 
     def kv_cols(g):
         return pl.ds(pl.multiple_of(g * PAIR, PAIR), PAIR)
@@ -90,21 +92,15 @@
             {"section": lax.rem(sec + 7, 8)},
         )
 
-    def send_az(shard, slot, there, to):
-        src = wall.at[shard * 4 + y]
-        return remote(src, src, az_s.at[slot], az_r.at[there], at(to, y))
-
-    def send_az_up():
-        return send_az(h, 0, 2, mod4(h + 1))
-
-    def send_az_down():
-        return send_az(h, 1, 0, mod4(h - 1))
-
-    def send_az_relay():
-        return send_az(mod4(h + 1), 2, 1, mod4(h - 1))
+    def send_az(away):
+        src = wall.at[p]
+        where = at(mod4(h - away), y)
+        if isinstance(away, int) and away == 2:
+            where["dp"] = mod4(l + 1)
+        return remote(src, src, az_s.at[away - 1], az_r.at[away - 1], where)
 
     def wait_az(away):
-        send_az(h, 0, away - 1, mod4(h + 1)).wait_recv()
+        send_az(away).wait_recv()
 
     def send_ay(g, d):
         shard = wall.at[g * 4 + y]
@@ -179,21 +175,22 @@
         to = mod4(y + d)
         return remote(ws.at[g, to], wr.at[g, d - 1], wy_s.at[g, d - 1], wy_r.at[g, d - 1], at(h, to))
 
-    def send_wl(g, d):
+    def send_wz(g, d):
         to = mod4(l + d)
-        return remote(
-            wz.at[g, pl.ds(pl.multiple_of(to * PART, PART), PART)], wl.at[g, d - 1],
-            wl_s.at[g, d - 1], wl_r.at[g, d - 1], {"dp": to},
-        )
-
-    def send_wh(g):
-        slot = mod4(h - g + 3)
-        return remote(wh.at[g], wf.at[slot], wh_s.at[g], wh_r.at[slot], at(g, y))
-
-    def wait_wh(slot):
-        remote(wh.at[0], wf.at[slot], wh_s.at[0], wh_r.at[slot], at(mod4(h + 1), y)).wait_recv()
+        slot = mod4(h - g) * 4 + mod4(-d)
+        where = at(g, y)
+        where["dp"] = to
+        return remote(
+            wz.at[g, pl.ds(pl.multiple_of(to * PART, PART), PART)], wf.at[slot],
+            wz_s.at[g, d], wz_r.at[slot], where,
+        )
+
+    def wait_wz(slot):
+        remote(wf.at[0], wf.at[slot], wz_s.at[0, 0], wz_r.at[slot], at(mod4(h + 1), y)).wait_recv()
 
     low_h = h < 3
+    early = (h == 0) | (h == 3)
+    late = (h == 1) | (h == 2)
     high_h = h > 0
 
     load_w().start()
@@ -212,6 +209,12 @@
     greet({"section": lax.rem(sec + 1, 8)})
     greet(at(mod4(h + 1), y))
     greet(at(mod4(h - 1), y))
+
+    @pl.when(early)
+    def _():
+        greet({"seq": mod4(h + 2) * 4 + y, "dp": mod4(l - 1)})
+        greet({"seq": mod4(h + 2) * 4 + y, "dp": mod4(l + 1)})
+
     for d in range(1, 4):
         greet(at(h, mod4(y + d)))
         greet({"dp": mod4(l + d)})
@@ -232,6 +235,72 @@
     @pl.when((y == 2) & low_h)
     def _():
         greet(at(h + 1, 1))
+
+    extra = (
+        jnp.where((y == 0) & high_h, 3, 0)
+        + jnp.where((y >= 1) & low_h, 1, 0)
+        + jnp.where((y == 1) & high_h, 1, 0)
+        + jnp.where((y == 2) & low_h, 1, 0)
+        + jnp.where(late, 2, 0)
+    )
+    pl.semaphore_wait(bar, 10 + extra)
+
+    @pl.when(late)
+    def _():
+        pl.semaphore_signal(
+            far_sem, inc=1, device_id={"seq": mod4(h + 2) * 4 + y, "dp": mod4(l - 1)},
+            device_id_type=MESH,
+        )
+
+
+    for g in range(4):
+        load_kv(g).wait()
+
+    @pl.when((y == 2) & low_h)
+    def _():
+        for j in range(4):
+            send_x1(group(j, h + 1), HALF, 1).start()
+
+    @pl.when((y == 3) & low_h)
+    def _():
+        for j in range(4):
+            send_x1(group(j, h + 1), 0, 0).start()
+
+    load_w().wait()
+    send_az(1).start()
+
+    @pl.when(late)
+    def _():
+        send_az(2).start()
+
+    send_az(3).start()
+    for d in (1, 3, 2):
+        send_ay(h, d).start()
+
+    @pl.when((y == 2) & low_h)
+    def _():
+        for j in range(4):
+            send_x2_own(group(j, h + 1), 0, 0, 2).start()
+
+    @pl.when((y == 3) & low_h)
+    def _():
+        for j in range(4):
+            send_x2_own(group(j, h + 1), HALF, 192, 3).start()
+
+    send_cot(group(0)).start()
+
+    for i in range(4):
+        g = group(i)
+        if i > 0:
+            send_cot(g).start()
+
+        @pl.when(y < 3)
+        def _():
+            send_n1(g).start()
+
+        @pl.when(y < 2)
+        def _():
+            send_n2(g).start()
 
     def docs(block):
         return doc_ref[0, :, pl.ds(pl.multiple_of(block * ROWS, ROWS), ROWS)].astype(F32)
@@ -268,51 +337,6 @@
 
     da_acc[...] = jnp.zeros((RANK, ROWS), F32)
 
-    extra = (
-        jnp.where((y == 0) & high_h, 3, 0)
-        + jnp.where((y >= 1) & low_h, 1, 0)
-        + jnp.where((y == 1) & high_h, 1, 0)
-        + jnp.where((y == 2) & low_h, 1, 0)
-    )
-    pl.semaphore_wait(bar, 10 + extra)
-
-    for g in range(4):
-        load_kv(g).wait()
-
-    @pl.when((y == 2) & low_h)
-    def _():
-        for j in range(4):
-            send_x1(group(j, h + 1), HALF, 1).start()
-        for j in range(4):
-            send_x2_own(group(j, h + 1), 0, 0, 2).start()
-
-    @pl.when((y == 3) & low_h)
-    def _():
-        for j in range(4):
-            send_x1(group(j, h + 1), 0, 0).start()
-        for j in range(4):
-            send_x2_own(group(j, h + 1), HALF, 192, 3).start()
-
-    load_w().wait()
-    for d in (1, 3, 2):
-        send_ay(h, d).start()
-    send_az_down().start()
-    send_cot(group(0)).start()
-    send_az_up().start()
-
-    for i in range(4):
-        g = group(i)
-        if i > 0:
-            send_cot(g).start()
-
-        @pl.when(y < 3)
-        def _():
-            send_n1(g).start()
-
-        @pl.when(y < 2)
-        def _():
-            send_n2(g).start()
-
     @pl.when((y == 1) & low_h)
     def _():
         for j in range(4):
@@ -327,16 +351,17 @@
             send_x1(g, 0, 0).wait_recv()
             send_x2_staged(g, 128, 0).start()
 
+    @pl.when(early)
+    def _():
+        pl.semaphore_wait(far_sem, 1)
+        send_az(2).start()
+
     def pass_shard(g):
         away = mod4(g - h)
 
         @pl.when(away > 0)
         def _():
             wait_az(away)
-
-            @pl.when(away == 1)
-            def _():
-                send_az_relay().start()
 
             for d in (1, 3, 2):
                 send_ay(g, d).start()
@@ -378,52 +403,34 @@
         w_g = jnp.concatenate([wall[g * 4 + k] for k in range(4)], axis=1)
         keys = kvw[i, :, :HEAD]
         values = kvw[i, :, HEAD:]
-        d_key = jnp.zeros((3 * ROWS, HEAD), F32)
-        d_value = jnp.zeros((3 * ROWS, HEAD), F32)
-        da = da_acc[...]
-        seen = bias[...]
-        seen = jnp.concatenate([seen] * CHUNK, axis=1)
-        for first in range(0, 8, CHUNK):
-            cols = slice(first * HEAD, (first + CHUNK) * HEAD)
-            w_cols = w_g[:, cols]
-            queries = (qf[i, :, cols].astype(F32) + dot(a_cols, w_cols, 0, 0)).astype(BF16)
-            cots = cot[i, :, cols]
-            q_rows = jnp.concatenate(
-                [queries[:, k * HEAD:(k + 1) * HEAD] for k in range(CHUNK)], axis=0
-            )
-            c_rows = jnp.concatenate(
-                [cots[:, k * HEAD:(k + 1) * HEAD] for k in range(CHUNK)], axis=0
-            )
-            scores = dot(keys, q_rows, 1, 1) * (SCALE * math.log2(math.e)) + seen
-            top = jnp.max(scores, axis=0, keepdims=True)
-            raised = jnp.exp2(scores - top)
-            probs = raised * (1.0 / jnp.sum(raised, axis=0, keepdims=True))
-            dprobs = dot(values, c_rows, 1, 1)
-            deltas = jnp.sum(probs * dprobs, axis=0, keepdims=True)
-            dscores = (probs * (dprobs - deltas)).astype(BF16)
-            d_value = d_value + dot(probs.astype(BF16), c_rows, 1, 0)
-            d_key = d_key + dot(dscores, q_rows, 1, 0)
-            dq_rows = (dot(dscores, keys, 0, 0) * SCALE).astype(BF16)
-            dq = jnp.concatenate(
-                [dq_rows[k * ROWS:(k + 1) * ROWS] for k in range(CHUNK)], axis=1
-            )
-            dqv[i, :, cols] = dq
-            da = da + dot(w_cols, dq, 1, 1)
-        da_acc[...] = da
+        seen = jnp.concatenate([bias[...]] * 8, axis=1)
+        queries = (qf[i].astype(F32) + dot(a_cols, w_g, 0, 0)).astype(BF16)
+        cots = cot[i]
+        q_rows = jnp.concatenate([queries[:, k * HEAD:(k + 1) * HEAD] for k in range(8)], axis=0)
+        c_rows = jnp.concatenate([cots[:, k * HEAD:(k + 1) * HEAD] for k in range(8)], axis=0)
+        scores = dot(keys, q_rows, 1, 1) * (SCALE * math.log2(math.e)) + seen
+        top = jnp.max(scores, axis=0, keepdims=True)
+        raised = jnp.exp2(scores - top)
+        probs = raised * (1.0 / jnp.sum(raised, axis=0, keepdims=True))
+        dprobs = dot(values, c_rows, 1, 1)
+        deltas = jnp.sum(probs * dprobs, axis=0, keepdims=True)
+        dscores = (probs * (dprobs - deltas)).astype(BF16)
+        d_value = dot(probs.astype(BF16), c_rows, 1, 0)
+        d_key = dot(dscores, q_rows, 1, 0)
         grads = jnp.concatenate([d_key * SCALE, d_value], axis=1)
         own[i] = grads[2 * ROWS:]
         dkvs[i] = grads[:2 * ROWS].astype(BF16)
 
         @pl.when((y == 0) & high_h)
         def _():
-            send_d1(i, 0, 0, 0, 2).start()
             send_d1(i, 64, 0, 1, 1).start()
             send_d1(i, 192, 0, 2, 3).start()
+            send_d1(i, 0, 0, 0, 2).start()
 
         @pl.when((y == 1) & high_h)
         def _():
+            send_d1(i, 64, 1, 1, 3).start()
             send_d1(i, 0, 0, 0, 0).start()
-            send_d1(i, 64, 1, 1, 3).start()
 
         @pl.when(y >= 1)
         def _():
@@ -433,11 +440,15 @@
         def _():
             send_m2(i).start()
 
-        dw = dot(a_cols, dqv[i], 1, 0).astype(BF16)
+        dq_rows = (dot(dscores, keys, 0, 0) * SCALE).astype(BF16)
+        dq = jnp.concatenate([dq_rows[k * ROWS:(k + 1) * ROWS] for k in range(8)], axis=1)
+        dqv[i] = dq
+        dw = dot(a_cols, dq, 1, 0).astype(BF16)
         for k in range(4):
             ws[i, k] = dw[:, k * 256:(k + 1) * 256]
         for d in (1, 3, 2):
             send_wy(i, d).start()
+        da_acc[...] += dot(w_g, dq, 1, 1)
 
     def second(r):
         i = group(r)
@@ -471,40 +482,24 @@
             total = total + wr[i, d - 1].astype(F32)
         wz[i] = total.astype(BF16)
         for d in (1, 3, 2):
-            send_wl(i, d).start()
-
-    def third(r):
-        i = group(r)
-        total = wz[i, pl.ds(pl.multiple_of(l * PART, PART), PART), :].astype(F32)
-        for d in range(1, 4):
-            send_wl(i, d).wait_recv()
-            total = total + wl[i, d - 1].astype(F32)
-
-        @pl.when(i == h)
-        def _():
-            w_own[...] = total
+            send_wz(i, d).start()
 
         @pl.when(i != h)
         def _():
-            wh[i] = total.astype(BF16)
-            send_wh(i).start()
+            send_wz(i, 0).start()
 
     def round_(r, _):
         @pl.when(r < 4)
         def _():
             work(r)
 
-        @pl.when((r >= 1) & (r < 5))
+        @pl.when(r >= 1)
         def _():
             second(r - 1)
 
-        @pl.when(r >= 2)
-        def _():
-            third(r - 2)
-
         return 0
 
-    lax.fori_loop(0, 6, round_, 0)
+    lax.fori_loop(0, 5, round_, 0)
 
     da_ref[...] = da_acc[...].astype(BF16)
 
@@ -533,26 +528,25 @@
         return 0
 
     lax.fori_loop(0, 4, settle, 0)
-    total = w_own[...]
-    for k in range(3):
-        wait_wh(k)
+    total = wz[h, pl.ds(pl.multiple_of(l * PART, PART), PART), :].astype(F32)
+    for k in range(1, 16):
+        wait_wz(k)
         total = total + wf[k].astype(F32)
     dw_ref[...] = total
 
-    send_az_up().wait_send()
-    send_az_down().wait_send()
-    send_az_relay().wait_send()
+    for away in range(1, 4):
+        send_az(away).wait_send()
 
     def drain(g, _):
         send_cot(g).wait_send()
         for d in range(1, 4):
             send_ay(g, d).wait_send()
             send_wy(g, d).wait_send()
-            send_wl(g, d).wait_send()
+            send_wz(g, d).wait_send()
 
         @pl.when(g != h)
         def _():
-            send_wh(g).wait_send()
+            send_wz(g, 0).wait_send()
 
         @pl.when(y < 3)
         def _():
@@ -633,17 +627,14 @@
         pltpu.VMEM((4, 4, RANK, 256), BF16),
         pltpu.VMEM((4, 3, RANK, 256), BF16),
         pltpu.VMEM((4, RANK, 256), BF16),
-        pltpu.VMEM((4, 3, PART, 256), BF16),
-        pltpu.VMEM((4, PART, 256), BF16),
-        pltpu.VMEM((3, PART, 256), BF16),
-        pltpu.VMEM((PART, 256), F32),
+        pltpu.VMEM((16, PART, 256), BF16),
         dma((4,)), dma((4,)), dma, dma,
         dma((4,)), dma((4,)), dma((3,)), dma((3,)), dma((4, 3)), dma((4, 3)),
         dma((4,)), dma((4,)), dma((4,)), dma((4,)), dma((4,)),
         dma((4,)), dma((4,)), dma((4,)), dma((4, 4)),
         dma((4,)), dma((4,)), dma((4,)), dma((4,)),
         dma((4, 3)), dma((4, 2)), dma((4,)), dma((4, 2)),
-        dma((4, 3)), dma((4, 3)), dma((4, 3)), dma((4, 3)), dma((4,)), dma((3,)),
+        dma((4, 3)), dma((4, 3)), dma((4, 4)), dma((16,)), pltpu.SemaphoreType.REGULAR,
     ]
     results = pl.pallas_call(
         kernel,
@@ -657,7 +648,7 @@
         out_specs=(vmem,) * 4,
         scratch_shapes=scratch,
         compiler_params=pltpu.CompilerParams(
-            collective_id=0, has_side_effects=True, vmem_limit_bytes=62 << 20
+            collective_id=0, has_side_effects=True, vmem_limit_bytes=54 << 20
         ),
     )(
         frozen_queries, key_value_pairs, jnp.swapaxes(adapter_input, 2, 3),
@@ -674,7 +665,7 @@
         in_specs=[vmem] * 4,
         out_specs=(hbm,) * 4,
         scratch_shapes=[dma((10,))],
-        compiler_params=pltpu.CompilerParams(vmem_limit_bytes=62 << 20),
+        compiler_params=pltpu.CompilerParams(vmem_limit_bytes=54 << 20),
     )(*results)
     return dq, dkv, jnp.swapaxes(da, 2, 3), dw
 

time: 70.9 us -> 68.6 us (0.968)
  the two profiles are of different devices: /device:TPU:12 before, /device:TPU:124 now
where the time goes in v3:
time: 68.6 us; the launch traced here: 68.4 us
  Pallas kernels  67.7 us (99%)
    pallas_call x1, Pallas kernels, per_device(): pl.pallas_call(kernel, out_shape=(jax.ShapeDtypeStruct((4, ROWS, WIDE), B...  65.3 us
    pallas_call x1, Pallas kernels, per_device(): pl.pallas_call(finish, out_shape=(jax.ShapeDtypeStruct((1, 1, ROWS, 4 * W...  2.45 us

profile of v3, /device:TPU:124, one launch (start us, length us, event | category | flops | bytes accessed | tf_op | source)
XLA Modules:
  0.0 68.4 jit_solution(2747239737576440732)
XLA Ops:
  0.6 65.3 %shard_map.93 = (bf16[4,128,1024]{2,1,0:T(8,128)(2,1)}, bf16[4,128,256]{2,1,0:T(8,128)(2,1)}, bf16[64,128]{1,0:T(8,128)(2,1)}, f32[16,256]{1,0:T(8,128)}) custom-call(bf16[1,1,128,4096]{3,2,1,0:T(8,128)(2,1)} %q_hbm.1, bf16[1,1,128,1024]{3,2,1,0:T(8,128)(2,1)} %kv_hbm.1, bf16[1,1,64,128]{3,2,1,0:T(8,128)(2,1)} %bitcast.2, bf16[1,64,256]{2,1,0:T(8,128)(2,1)} %w_hbm.1, ...), custom_call_target="tpu_custom_call" | custom-call | tf_op jit(solution)/shard_map/pallas_call | solution.py:639
  65.9 2.4 %shard_map.94 = (bf16[1,1,128,4096]{3,2,1,0:T(8,128)(2,1)}, bf16[1,1,128,1024]{3,2,1,0:T(8,128)(2,1)}, bf16[1,1,64,128]{3,2,1,0:T(8,128)(2,1)}, f32[1,16,256]{2,1,0:T(8,128)}) custom-call(bf16[4,128,1024]{2,1,0:T(8,128)(2,1)} %get-tuple-element.12.dq_ref, bf16[4,128,256]{2,1,0:T(8,128)(2,1)} %get-tuple-element.13.dkv_ref, ...), custom_call_target="tpu_custom_call" | custom-call | tf_op jit(solution)/shard_map/pallas_call | solution.py:657

commit v4 on v3

--- a/solution.py
+++ b/solution.py
@@ -501,6 +501,53 @@
 
     lax.fori_loop(0, 5, round_, 0)
 
+    for away in range(1, 4):
+        send_az(away).wait_send()
+
+    def drain(g, _):
+        send_cot(g).wait_send()
+        for d in range(1, 4):
+            send_ay(g, d).wait_send()
+            send_wy(g, d).wait_send()
+
+        @pl.when(y < 3)
+        def _():
+            send_n1(g).wait_send()
+
+        @pl.when(y < 2)
+        def _():
+            send_n2(g).wait_send()
+
+        @pl.when((y >= 2) & low_h)
+        def _():
+            send_x1(g, 0, 0).wait_send()
+
+        @pl.when(low_h)
+        def _():
+            send_x2_staged(g, 0, 0).wait_send()
+
+        @pl.when(y >= 1)
+        def _():
+            send_m1(g).wait_send()
+
+        @pl.when(y >= 2)
+        def _():
+            send_m2(g).wait_send()
+
+        @pl.when((y < 2) & high_h)
+        def _():
+            send_d1(g, 0, 0, 0, 0).wait_send()
+            send_d1(g, 0, 0, 1, 0).wait_send()
+
+        @pl.when((y == 0) & high_h)
+        def _():
+            send_d1(g, 0, 0, 2, 0).wait_send()
+            send_fwd(g).wait_send()
+
+        return 0
+
+    lax.fori_loop(0, 4, drain, 0)
+
     da_ref[...] = da_acc[...].astype(BF16)
 
     def settle(r, _):
@@ -534,61 +581,21 @@
         total = total + wf[k].astype(F32)
     dw_ref[...] = total
 
-    for away in range(1, 4):
-        send_az(away).wait_send()
-
-    def drain(g, _):
-        send_cot(g).wait_send()
+    def drain_last(g, _):
         for d in range(1, 4):
-            send_ay(g, d).wait_send()
-            send_wy(g, d).wait_send()
             send_wz(g, d).wait_send()
 
         @pl.when(g != h)
         def _():
             send_wz(g, 0).wait_send()
 
-        @pl.when(y < 3)
-        def _():
-            send_n1(g).wait_send()
-
-        @pl.when(y < 2)
-        def _():
-            send_n2(g).wait_send()
-
-        @pl.when((y >= 2) & low_h)
-        def _():
-            send_x1(g, 0, 0).wait_send()
-
-        @pl.when(low_h)
-        def _():
-            send_x2_staged(g, 0, 0).wait_send()
-
-        @pl.when(y >= 1)
-        def _():
-            send_m1(g).wait_send()
-
-        @pl.when(y >= 2)
-        def _():
-            send_m2(g).wait_send()
-
-        @pl.when((y < 2) & high_h)
-        def _():
-            send_d1(g, 0, 0, 0, 0).wait_send()
-            send_d1(g, 0, 0, 1, 0).wait_send()
-
-        @pl.when((y == 0) & high_h)
-        def _():
-            send_d1(g, 0, 0, 2, 0).wait_send()
-            send_fwd(g).wait_send()
-
         @pl.when(high_h)
         def _():
             send_d2(g, ds.at[g, 0], 0, 0, 2).wait_send()
 
         return 0
 
-    lax.fori_loop(0, 4, drain, 0)
+    lax.fori_loop(0, 4, drain_last, 0)
 
 
 def finish(dq_ref, dkv_ref, da_ref, dw_ref, dq_hbm, dkv_hbm, da_hbm, dw_hbm, sems):

time: 68.6 us -> 68.5 us (level)
  no operation moved by 1% of the time
where the time goes in v4:
time: 68.5 us; the launch traced here: 68.3 us
  Pallas kernels  67.6 us (99%)
    pallas_call x1, Pallas kernels, per_device(): pl.pallas_call(kernel, out_shape=(jax.ShapeDtypeStruct((4, ROWS, WIDE), B...  65.2 us
    pallas_call x1, Pallas kernels, per_device(): pl.pallas_call(finish, out_shape=(jax.ShapeDtypeStruct((1, 1, ROWS, 4 * W...  2.45 us

profile of v4, /device:TPU:124, one launch (start us, length us, event | category | flops | bytes accessed | tf_op | source)
XLA Modules:
  0.0 68.3 jit_solution(110148462191688962)
XLA Ops:
  0.6 65.2 %shard_map.93 = (bf16[4,128,1024]{2,1,0:T(8,128)(2,1)}, bf16[4,128,256]{2,1,0:T(8,128)(2,1)}, bf16[64,128]{1,0:T(8,128)(2,1)}, f32[16,256]{1,0:T(8,128)}) custom-call(bf16[1,1,128,4096]{3,2,1,0:T(8,128)(2,1)} %q_hbm.1, bf16[1,1,128,1024]{3,2,1,0:T(8,128)(2,1)} %kv_hbm.1, bf16[1,1,64,128]{3,2,1,0:T(8,128)(2,1)} %bitcast.2, bf16[1,64,256]{2,1,0:T(8,128)(2,1)} %w_hbm.1, ...), custom_call_target="tpu_custom_call" | custom-call | tf_op jit(solution)/shard_map/pallas_call | solution.py:646
  65.8 2.4 %shard_map.94 = (bf16[1,1,128,4096]{3,2,1,0:T(8,128)(2,1)}, bf16[1,1,128,1024]{3,2,1,0:T(8,128)(2,1)}, bf16[1,1,64,128]{3,2,1,0:T(8,128)(2,1)}, f32[1,16,256]{2,1,0:T(8,128)}) custom-call(bf16[4,128,1024]{2,1,0:T(8,128)(2,1)} %get-tuple-element.12.dq_ref, bf16[4,128,256]{2,1,0:T(8,128)(2,1)} %get-tuple-element.13.dkv_ref, ...), custom_call_target="tpu_custom_call" | custom-call | tf_op jit(solution)/shard_map/pallas_call | solution.py:664
